TPU v7x, 32 devices: a whole 2x2x4 slice. The times are simulated.
32 devices in a mesh: batch: 4 (over x, core), row: 4 (over z), col: 2 (over y).
Axes of the slice: x: 2, y: 2, z: 4, core: 2. Of those that a mesh axis runs over, the one named last changes fastest.
Arguments:
- tokens: bfloat16 [16, 112, 56, 256], P('batch', 'row', 'col'), may hold values from -6 to 6
- heights: int32 [16], P('batch'), may hold values from 57 to 112, as said below
- widths: int32 [16], P('batch'), may hold values from 29 to 56, as said below
- keep_flags: int32 [16, 2], P('batch'), may hold values from 0 to 1, as said below
- out_grad: bfloat16 [16, 112, 56, 256], P('batch', 'row', 'col'), may hold values from -6 to 6
- first_gain: float32 [256], replicated, may hold values from 0.5 to 1.5
- first_shift: float32 [256], replicated, may hold values from -2 to 2
- triple_weight: bfloat16 [256, 768], replicated, may hold values from -0.375 to 0.375
- query_value_bias: float32 [2, 256], replicated, may hold values from -3 to 3
- position_kernel: float32 [3, 3, 256], replicated, may hold values from -1 to 1
- position_bias: float32 [256], replicated, may hold values from -2 to 2
- mixing_weight: bfloat16 [256, 256], replicated, may hold values from -1.5 to 1.5
- mixing_bias: float32 [256], replicated, may hold values from -2 to 2
- second_gain: float32 [256], replicated, may hold values from 0.5 to 1.5
- second_shift: float32 [256], replicated, may hold values from -2 to 2
- expand_weight: bfloat16 [256, 1024], replicated, may hold values from -0.375 to 0.375
- expand_bias: float32 [1024], replicated, may hold values from -3 to 3
- reduce_weight: bfloat16 [1024, 256], replicated, may hold values from -0.1875 to 0.1875
- reduce_bias: float32 [256], replicated, may hold values from -2 to 2
Outputs:
- output: bfloat16 [16, 112, 56, 256], P('batch', 'row', 'col')
- tokens_grad: bfloat16 [16, 112, 56, 256], P('batch', 'row', 'col')
- first_gain_grad: float32 [256], replicated
- first_shift_grad: float32 [256], replicated
- triple_weight_grad: float32 [256, 768], replicated
- query_value_bias_grad: float32 [2, 256], replicated
- position_kernel_grad: float32 [3, 3, 256], replicated
- position_bias_grad: float32 [256], replicated
- mixing_weight_grad: float32 [256, 256], replicated
- mixing_bias_grad: float32 [256], replicated
- second_gain_grad: float32 [256], replicated
- second_shift_grad: float32 [256], replicated
- expand_weight_grad: float32 [256, 1024], replicated
- expand_bias_grad: float32 [1024], replicated
- reduce_weight_grad: float32 [1024, 256], replicated
- reduce_bias_grad: float32 [256], replicated
Inputs may be any that keep to these rules, and one draw needn't show every extreme that they name: `heights`: in every group of 4 consecutive images one image has the full height 112 and the full width 56. `widths`: the image of full height is also of full width 56. `keep_flags`: the image of full size in each group of 4 consecutive images is kept in both columns.
All inputs are finite; a program needn't handle non-finite values.
Results may differ from a plain program's by a relative error of at most 0.012.
Values may be sent and summed in bfloat16 or wider, within the bound.
No kernel may reach another device: no remote copies, remote signals or barrier semaphores. Data moves between devices by JAX's collectives and lax.ppermute only.
A program may use at most 256 MiB of HBM per device.

v0:
```python
import functools

import jax
import jax.numpy as jnp
from jax import lax
from jax.experimental import pallas as pl
from jax.experimental.pallas import tpu as pltpu
from jax.sharding import PartitionSpec as P

DIM = 256
HALF = 128
HEADS = 4
SIZE = 32
STRIPE = 7
ROWS = 28
SLOT = 8
PIX = ROWS * SLOT
HIDDEN = 1024
VEC = DIM
PACKED = 3 * DIM + HALF
F32 = jnp.float32
BF16 = jnp.bfloat16
LOG2E = 1.4426950408889634
SCALE = SIZE**-0.5
EPS = 1e-05
GELU_C = 0.7978845608028654
GELU_A = 0.044715
VMEM_LIMIT = 56 * 1024 * 1024


def nn(a, b):
    return lax.dot_general(a, b, (((1,), (0,)), ((), ())), preferred_element_type=F32)


def nt(a, b):
    return lax.dot_general(a, b, (((1,), (1,)), ((), ())), preferred_element_type=F32)


def tn(a, b):
    return lax.dot_general(a, b, (((0,), (0,)), ((), ())), preferred_element_type=F32)


def col_sum(v):
    return jnp.sum(v, axis=0, keepdims=True)


def normalize(source):
    average = jnp.mean(source, axis=-1, keepdims=True)
    centered = source - average
    spread = jnp.mean(centered * centered, axis=-1, keepdims=True)
    rstd = lax.rsqrt(spread + EPS)
    return centered * rstd, rstd


def norm_back(grad_hat, hat, rstd):
    return rstd * (
        grad_hat
        - jnp.mean(grad_hat, axis=-1, keepdims=True)
        - hat * jnp.mean(grad_hat * hat, axis=-1, keepdims=True)
    )


def head_lanes(shape):
    return lax.broadcasted_iota(jnp.int32, shape, len(shape) - 1) // SIZE


def split_cols(source, wide, parts):
    wide[:, 0:ROWS, :] = source.astype(F32)
    slot = lax.broadcasted_iota(jnp.int32, (ROWS, SLOT, DIM), 1)
    for s in range(4):
        parts[s] = jnp.where(slot < STRIPE, wide[:, STRIPE * s : STRIPE * s + SLOT, :], 0.0)


def merge_cols(parts, wide):
    for s in range(4):
        wide[:, STRIPE * s : STRIPE * s + SLOT, :] = parts[s]
    return wide[:, 0:ROWS, :]


class Meta:
    def __init__(self, ref, count):
        self.ref = ref
        self.count = count

    def height(self, i):
        return self.ref[i]

    def width(self, i):
        return self.ref[self.count + i]

    def keep(self, i):
        return self.ref[2 * self.count + i]

    def feed(self, i):
        return self.ref[3 * self.count + i]

    def row(self):
        return self.ref[4 * self.count]

    def col(self):
        return self.ref[4 * self.count + 1]


def pair_start(owner):
    return 2 * (1 - owner)


def from_rows(refs, r, out):
    for k, ref in enumerate(refs):
        out[lax.rem(r + 4 - k, 4)] = ref[0]


def to_rows(refs, r, source):
    for k, ref in enumerate(refs):
        ref[0] = source[lax.rem(r + k, 4)]


def own_stripes(keep_ref, other_ref, c):
    for ref, owner in ((keep_ref, c), (other_ref, 1 - c)):
        for u in range(2):
            yield pl.ds(STRIPE * (pair_start(owner) + u), STRIPE), ref.at[0, u]


def fetch(source, target, sem):
    return pltpu.make_async_copy(source, target, sem)


def prep_kernel(count, first, meta_ref, tok_ref, d0, d1, d2, d3, keep_ref, send_ref, wide, parts):
    meta = Meta(meta_ref, count)
    split_cols(tok_ref[0], wide, parts)
    r, c = meta.row(), meta.col()
    for k, ref in enumerate((d0, d1, d2, d3)):
        ref[0] = parts[lax.rem(r + k, 4)].reshape(PIX, DIM).astype(BF16)
    for where, ref in own_stripes(keep_ref, send_ref, c):
        ref[...] = parts[:, where].reshape(PIX, DIM).astype(BF16)


def down_mask(height, width, stripe):
    shape = (4 * ROWS, SLOT, HALF)
    row = lax.broadcasted_iota(jnp.int32, shape, 0)
    j = lax.broadcasted_iota(jnp.int32, shape, 1)
    limit = jnp.minimum(STRIPE, width - STRIPE * stripe)
    return jnp.where((row < height) & (j < limit), 1.0, 0.0)


def across_mask(height, width, stripe):
    shape = (2, 8, STRIPE, SLOT, HALF)
    u = lax.broadcasted_iota(jnp.int32, shape, 0)
    b = lax.broadcasted_iota(jnp.int32, shape, 1)
    row = lax.broadcasted_iota(jnp.int32, shape, 2)
    j = lax.broadcasted_iota(jnp.int32, shape, 3)
    good = (STRIPE * u + row < height - STRIPE * stripe) & (j < STRIPE) & (b * STRIPE + j < width)
    return jnp.where(good, 1.0, 0.0)


def down_flags(height, width, stripe):
    at = lax.broadcasted_iota(jnp.int32, (16, PIXELS), 1)
    limit = jnp.minimum(STRIPE, width - STRIPE * stripe)
    good = (at < SLOT * height) & (lax.rem(at, SLOT) < limit)
    return jnp.where(good, 1.0, 0.0).astype(BF16)


def across_flags(height, width, stripe):
    at = lax.broadcasted_iota(jnp.int32, (16, PIXELS), 1)
    size = STRIPE * SLOT
    u = jnp.where(at < PIXELS // 2, 0, 1)
    b = jnp.zeros_like(at)
    for k in range(1, 16):
        b = jnp.where(at >= size * k, k, b)
    rest = at - size * b
    j = lax.rem(rest, SLOT)
    row = (rest - j) // SLOT + STRIPE * u
    col = STRIPE * (b - SLOT * u) + j
    good = (row < height - STRIPE * stripe) & (j < STRIPE) & (col < width)
    return jnp.where(good, 1.0, 0.0).astype(BF16)


def moved_rows(v, axis, step):
    if step == 0:
        return v
    size = v.shape[axis]
    zero_shape = v.shape[:axis] + (1,) + v.shape[axis + 1 :]
    zero = jnp.zeros(zero_shape, v.dtype)
    if step > 0:
        return jnp.concatenate([lax.slice_in_dim(v, 1, size, axis=axis), zero], axis=axis)
    return jnp.concatenate([zero, lax.slice_in_dim(v, 0, size - 1, axis=axis)], axis=axis)


def roll8(v, shift):
    shape = v.shape
    flat = v.reshape(-1, SLOT, HALF)
    return pltpu.roll(flat, shift, 1).reshape(shape)


def moved_cols_down(v, step):
    if step == 0:
        return v
    return roll8(v, 1 if step < 0 else SLOT - 1)


def moved_cols_across(v, step):
    if step == 0:
        return v
    slot = lax.broadcasted_iota(jnp.int32, v.shape, 3)
    if step < 0:
        return jnp.where(slot == 0, moved_rows(roll8(v, 2), 1, -1), roll8(v, 1))
    return jnp.where(slot == STRIPE - 1, moved_rows(roll8(v, SLOT - 2), 1, 1), roll8(v, SLOT - 1))


def taps(v, across):
    moved_cols = moved_cols_across if across else moved_cols_down
    row_axis = 2 if across else 0
    for b in range(3):
        side = moved_cols(v, b - 1)
        for a in range(3):
            yield a, b, moved_rows(side, row_axis, a - 1)


def position_term(v, kern_ref, bias_ref, lanes, across):
    total = bias_ref[0:1, lanes]
    for a, b, moved in taps(v, across):
        total = total + moved * kern_ref[3 * a + b : 3 * a + b + 1, lanes]
    return total


def position_back(grad, v, kern_ref, lanes, across):
    total = 0.0
    for a, b, moved in taps(grad, across):
        k = 3 * (2 - a) + (2 - b)
        total = total + moved * kern_ref[k : k + 1, lanes]
    kernel_grads = []
    flat = grad.reshape(-1, HALF)
    found = {}
    for a, b, moved in taps(v, across):
        found[3 * a + b] = col_sum(flat * moved.reshape(-1, HALF))
    for k in range(9):
        kernel_grads.append(found[k])
    return total, kernel_grads, col_sum(flat)


DOWN_GRID = (4 * ROWS, SLOT, HALF)
ACROSS_GRID = (2, 8, STRIPE, SLOT, HALF)
DOWN_SIZES = (640, 768, 896)
ACROSS_SIZES = (336, 448)
DOWN_GROUP = 4
MIDDLE_GROUP = 4
HIDDEN_TILE = 512
DOWN_BACK_GROUP = 2
PIXELS = 4 * PIX


def by_size(used, sizes, body):
    below = None
    for n in sizes:
        fits = used <= n
        if n == sizes[-1]:
            fits = True if below is None else used > below
        elif below is not None:
            fits = fits & (used > below)
        pl.when(fits)(functools.partial(body, n))
        below = n


def project(x_ref, weight_ref, bias_ref, gain_ref, shift_ref):
    hat, unused = normalize(x_ref[...].reshape(PIXELS, DIM).astype(F32))
    normed = (hat * gain_ref[...] + shift_ref[...]).astype(BF16)
    return (nn(normed, weight_ref[...]) + bias_ref[...]).astype(BF16)


def split_queries(query):
    scaled = query.astype(F32) * (SCALE * LOG2E)
    high = scaled.astype(BF16)
    low = (scaled - high.astype(F32)).astype(BF16)
    return jnp.concatenate([high, low], axis=1)


def valid_keys(keys, mask, stripes):
    size = PIXELS // stripes
    keys = keys.astype(F32)
    fixed = [
        jnp.where(
            mask[size * u : size * u + size] > 0.0, keys[size * u : size * u + size], keys[size * u : size * u + 1]
        )
        for u in range(stripes)
    ]
    return jnp.concatenate(fixed, axis=0).astype(BF16)


def only_head(value, h):
    lane = lax.broadcasted_iota(jnp.int32, value.shape, 1)
    return jnp.where(lax.rem(lane, HALF) // SIZE == h, value, jnp.zeros_like(value))


def attend(key_ref, query_ref, turned_ref, base, at_out, lse_out, a_ref, turned_a, full, group, n):
    part = pl.ds(base, n)
    whole_part = pl.ds(base, full)

    def heads_of(t, carry):
        heads = [t * group + j for j in range(group)]
        keys = key_ref[part]
        keys = jnp.concatenate([keys, keys], axis=1)
        queries = query_ref[part]
        scores = [nt(keys, only_head(queries, h)) for h in heads]
        tops = [jnp.max(s, axis=0, keepdims=True) for s in scores]
        weights = [jnp.exp2(s - top).astype(BF16) for s, top in zip(scores, tops)]
        outs = [nn(turned_ref[h, :, 0:n], w) for h, w in zip(heads, weights)]
        for h, out, top in zip(heads, outs, tops):
            total = out[SIZE : SIZE + 1]
            turned_a[pl.ds(pl.multiple_of(h * SIZE, SIZE), SIZE), 0:n] = out[0:SIZE] / total
            lse_out[pl.ds(h, 1), 0:n] = top + jnp.log2(total)
        return carry

    if group == HEADS:
        heads_of(0, 0)
    else:
        lax.fori_loop(0, HEADS // group, heads_of, 0)
    if n < full:
        a_ref[whole_part] = jnp.zeros((full, HALF), F32)
    at_out[:, 0:n] = turned_a[:, 0:n].astype(BF16)
    a_ref[part] = turned_a[:, 0:n].T


def prepare_forward(x_ref, mask, flags, stripes, weight_ref, bias_ref, gain_ref, shift_ref, saved, key_ref, query_ref, turned_ref):
    triple = project(x_ref, weight_ref, bias_ref, gain_ref, shift_ref)
    for k in range(3):
        saved[k] = triple[:, HALF * k : HALF * k + HALF]
    query_ref[...] = split_queries(triple[:, 0:HALF])
    key_ref[...] = valid_keys(triple[:, HALF : 2 * HALF], mask, stripes)
    masked = triple[:, 2 * HALF :].astype(F32) * mask
    turned = masked.astype(BF16).T
    size = PIXELS // stripes
    for u in range(stripes):
        part = slice(size * u, size * u + size)
        for h in range(HEADS):
            turned_ref[u, h, 0:SIZE] = turned[SIZE * h : SIZE * h + SIZE, part]
            turned_ref[u, h, SIZE:] = flags[:, part]
    return masked


def down_used(height):
    return SLOT * height


def live_stripes(height, stripe):
    return jnp.where(STRIPE * (stripe + 1) < height, 2, 1)


def across_used(width):
    return STRIPE * SLOT * ((width + STRIPE - 1) // STRIPE)


def forward_down_kernel(count, first, meta_ref, xd0, xd1, xd2, xd3, weight_ref, bias_ref, gain_ref, shift_ref,
                        kern_ref, pos_ref, jd0, jd1, jd2, jd3, q_out, k_out, v_out, at_out, lse_out,
                        x_ref, key_ref, query_ref, turned_ref, a_ref, j_ref, turned_a, saved, sems):
    meta = Meta(meta_ref, count)
    place = pl.program_id(0)
    i = first + place
    r, c = meta.row(), meta.col()
    height, width = meta.height(i), meta.width(i)
    stripe = 4 * c + r
    live = (meta.keep(i) > 0) & (STRIPE * stripe < width)

    @pl.when(live)
    def _():
        from_rows((xd0, xd1, xd2, xd3), r, x_ref)
        mask = down_mask(height, width, stripe)
        masked = prepare_forward(
            x_ref, mask.reshape(PIXELS, HALF), down_flags(height, width, stripe), 1, weight_ref, bias_ref, gain_ref, shift_ref,
            saved, key_ref, query_ref, turned_ref)
        copies = [fetch(saved.at[k], out.at[place], sems.at[k]) for k, out in enumerate((q_out, k_out, v_out))]
        for copy in copies:
            copy.start()

        def size(n):
            attend(key_ref, query_ref, turned_ref.at[0], 0, at_out.at[0], lse_out.at[0], a_ref, turned_a, PIXELS, DOWN_GROUP, n)

        by_size(down_used(height), DOWN_SIZES, size)
        term = position_term(masked.reshape(DOWN_GRID), kern_ref, pos_ref, slice(HALF, DIM), False)
        total = a_ref[...] + term.reshape(PIXELS, HALF)
        j_ref[...] = total.astype(BF16).reshape(4, PIX, HALF)
        to_rows((jd0, jd1, jd2, jd3), r, j_ref)
        for copy in copies:
            copy.wait()

    @pl.when(jnp.logical_not(live))
    def _():
        for ref in (jd0, jd1, jd2, jd3):
            ref[...] = jnp.zeros_like(ref)


def forward_across_kernel(count, first, meta_ref, xa_keep, xa_recv, weight_ref, bias_ref, gain_ref, shift_ref,
                          kern_ref, pos_ref, ja_keep, ja_send, q_out, k_out, v_out, at_out, lse_out,
                          x_ref, key_ref, query_ref, turned_ref, a_ref, j_ref, turned_a, saved, sems):
    meta = Meta(meta_ref, count)
    i = first + pl.program_id(0)
    place = i
    r, c = meta.row(), meta.col()
    height, width = meta.height(i), meta.width(i)
    stripe = 4 * r + pair_start(c)
    live = (meta.keep(i) > 0) & (STRIPE * stripe < height)

    @pl.when(live)
    def _():
        mask = across_mask(height, width, stripe)
        for u in range(2):
            x_ref[2 * u + c] = xa_keep[0, u]
            x_ref[2 * u + 1 - c] = xa_recv[0, u]
        masked = prepare_forward(
            x_ref, mask.reshape(PIXELS, HALF), across_flags(height, width, stripe), 2, weight_ref, bias_ref, gain_ref, shift_ref,
            saved, key_ref, query_ref, turned_ref)
        copies = [fetch(saved.at[k], out.at[place], sems.at[k]) for k, out in enumerate((q_out, k_out, v_out))]
        for copy in copies:
            copy.start()
        half = PIXELS // 2
        a_ref[half:] = jnp.zeros((half, HALF), F32)

        def stripe_of(u, carry):
            def size(n):
                base = pl.multiple_of(u * half, half)
                attend(key_ref, query_ref, turned_ref.at[u], base, at_out.at[0, u], lse_out.at[0, u], a_ref, turned_a, half, HEADS, n)

            by_size(across_used(width), ACROSS_SIZES, size)
            return carry

        lax.fori_loop(0, live_stripes(height, stripe), stripe_of, 0)
        term = position_term(masked.reshape(ACROSS_GRID), kern_ref, pos_ref, slice(0, HALF), True)
        j_ref[...] = (a_ref[...] + term.reshape(PIXELS, HALF)).astype(BF16).reshape(4, PIX, HALF)
        for u in range(2):
            ja_keep[0, u] = j_ref[2 * u + c]
            ja_send[0, u] = j_ref[2 * u + 1 - c]
        for copy in copies:
            copy.wait()

    @pl.when(jnp.logical_not(live))
    def _():
        ja_keep[...] = jnp.zeros_like(ja_keep)
        ja_send[...] = jnp.zeros_like(ja_send)


def pixel_mask(height, width, first_block, blocks, r, c):
    shape = (blocks, ROWS, SLOT, HALF)
    s = lax.broadcasted_iota(jnp.int32, shape, 0) + first_block
    row = lax.broadcasted_iota(jnp.int32, shape, 1)
    j = lax.broadcasted_iota(jnp.int32, shape, 2)
    good = (row < height - ROWS * r) & (j < STRIPE) & (s * STRIPE + j < width - ROWS * c)
    mask = jnp.where(good, 1.0, 0.0).reshape(blocks * PIX, HALF)
    return jnp.concatenate([mask, mask], axis=1)


def gelu_pair(pre, d_act):
    square = pre * pre
    bend = jnp.tanh(pre * (GELU_C + (GELU_C * GELU_A) * square))
    half_one = 0.5 + 0.5 * bend
    slope = half_one + (0.5 * pre) * (1.0 - bend * bend) * (GELU_C + (3.0 * GELU_C * GELU_A) * square)
    return (pre * half_one).astype(BF16), (d_act * slope).astype(BF16)


def middle_kernel(count, first, meta_ref, fact_ref, xd0, xd1, xd2, xd3, jd0, jd1, jd2, jd3, ja_keep, ja_recv, grad_ref,
                  wm_ref, bm_ref, gain_ref, shift_ref, we_ref, be_ref, wr_ref, br_ref, *rest):
    if first > 0:
        start, start_v, *rest = rest
        *rest, early, sem = rest
    (out_ref, dm_ref, dd0, dd1, dd2, dd3, da_keep, da_send, acc_out, acc_v, acc,
     x_ref, g_ref, ja_ref, j_ref, o_ref, dj_ref, wide) = rest
    meta = Meta(meta_ref, count)
    step = pl.program_id(0)
    i = first + step
    r, c = meta.row(), meta.col()
    height, width = meta.height(i), meta.width(i)
    attend_factor = fact_ref[2 * i]
    feed_factor = fact_ref[2 * i + 1]

    @pl.when(step == 0)
    def _():
        if first > 0:
            fetch(start, early, sem).start()
        acc[...] = jnp.zeros_like(acc)
        acc_v[...] = start_v[...] if first > 0 else jnp.zeros_like(acc_v)

    split_cols(grad_ref[0], wide, g_ref)
    for k, (xs, js) in enumerate(((xd0, jd0), (xd1, jd1), (xd2, jd2), (xd3, jd3))):
        x_ref[lax.rem(r + k, 4)] = xs[0]
        j_ref[lax.rem(r + 4 - k, 4), :, HALF:] = js[0]
    for where, ref in own_stripes(ja_keep, ja_recv, c):
        ja_ref[:, where] = ref[...].astype(F32).reshape(4, STRIPE, SLOT, HALF)
    j_ref[:, :, 0:HALF] = ja_ref[...].reshape(4, PIX, HALF).astype(BF16)

    group = MIDDLE_GROUP
    size = group * PIX

    def one(b, carry):
        where = pl.ds(group * b, group)
        mask = pixel_mask(height, width, group * b, group, r, c)
        scale_attend = mask * attend_factor
        scale_feed = mask * feed_factor
        x = x_ref[where].reshape(size, DIM).astype(F32)
        joined = j_ref[where].reshape(size, DIM)
        g = g_ref[where].reshape(size, DIM)
        mixed = nn(joined, wm_ref[...]) + bm_ref[...]
        middle = x + scale_attend * mixed
        hat, rstd = normalize(middle)
        normed = (hat * gain_ref[...] + shift_ref[...]).astype(BF16)
        d_reduced = (scale_feed * g).astype(BF16)
        turned_grad, turned_normed = d_reduced.T, normed.T
        tiles = HIDDEN // HIDDEN_TILE
        first_dots, hidden = {}, {}
        reduced, d_normed, sums = br_ref[...], 0.0, []
        for t in range(tiles + 2):
            if t < tiles:
                cols = slice(HIDDEN_TILE * t, HIDDEN_TILE * t + HIDDEN_TILE)
                first_dots[t] = nn(normed, we_ref[:, cols]), nt(d_reduced, wr_ref[cols])
            if 1 <= t <= tiles:
                j = t - 1
                cols = slice(HIDDEN_TILE * j, HIDDEN_TILE * j + HIDDEN_TILE)
                pre, d_act = first_dots.pop(j)
                hidden[j] = gelu_pair(pre + be_ref[:, cols], d_act)
            if t >= 2:
                j = t - 2
                cols = slice(HIDDEN_TILE * j, HIDDEN_TILE * j + HIDDEN_TILE)
                wide_cols = slice(HIDDEN + HIDDEN_TILE * j, HIDDEN + HIDDEN_TILE * j + HIDDEN_TILE)
                act, d_hidden = hidden.pop(j)
                reduced = reduced + nn(act, wr_ref[cols])
                d_normed = d_normed + nt(d_hidden, we_ref[:, cols])
                acc[:, cols] += nn(turned_grad, act)
                acc[:, wide_cols] += nn(turned_normed, d_hidden)
                sums.append(col_sum(d_hidden.astype(F32)))
        d_hidden_sum = jnp.concatenate(sums, axis=1)
        o_ref[where] = (middle + scale_feed * reduced).reshape(group, ROWS, SLOT, DIM)
        d_middle = g + norm_back(d_normed * gain_ref[...], hat, rstd)
        dm_ref[0, where] = d_middle.astype(BF16).reshape(group, PIX, DIM)
        d_mixed = (scale_attend * d_middle).astype(BF16)
        acc[:, 2 * HIDDEN :] += tn(joined, d_mixed)
        dj_ref[where] = nt(d_mixed, wm_ref[...]).reshape(group, ROWS, SLOT, DIM)
        rows = [d_hidden_sum[:, DIM * k : DIM * k + DIM] for k in range(4)]
        rows.append(col_sum(d_reduced.astype(F32)))
        rows.append(col_sum(d_normed * hat))
        rows.append(col_sum(d_normed))
        rows.append(col_sum(d_mixed.astype(F32)))
        acc_v[...] += jnp.concatenate(rows, axis=0)
        return carry

    lax.fori_loop(0, 4 // group, one, 0)

    @pl.when(step == pl.num_programs(0) - 1)
    def _():
        if first > 0:
            fetch(start, early, sem).wait()
            acc_out[...] = (acc[...] + early[...].astype(F32)).astype(BF16)
        else:
            acc_out[...] = acc[...].astype(BF16)

    out_ref[0] = merge_cols(o_ref, wide).astype(BF16)
    for k, ref in enumerate((dd0, dd1, dd2, dd3)):
        ref[0] = dj_ref[lax.rem(r + k, 4), :, :, HALF:].reshape(PIX, HALF).astype(BF16)
    for where, ref in own_stripes(da_keep, da_send, c):
        ref[...] = dj_ref[:, where, :, 0:HALF].reshape(PIX, HALF).astype(BF16)


def attend_back(key_ref, query_ref, q_ref, v_ref, turned_ref, up_ref, at_ref, lse_ref, base,
                delta_ref, dqt_ref, dq_ref, dk_ref, dv_ref, full, group, n):
    part = pl.ds(base, n)
    whole_part = pl.ds(base, full)
    product = up_ref[part].T.astype(F32) * at_ref[:, 0:n].astype(F32)
    for h in range(HEADS):
        delta_ref[h : h + 1, 0:n] = col_sum(product[SIZE * h : SIZE * h + SIZE])
    dk_ref[whole_part] = jnp.zeros((full, HALF), F32)

    def heads_of(t, carry):
        heads = [t * group + j for j in range(group)]
        keys = key_ref[part]
        keys = jnp.concatenate([keys, keys], axis=1)
        scaled, queries, values, up = query_ref[part], q_ref[part], v_ref[part], up_ref[part]
        ups = jnp.concatenate([only_head(up, h) for h in heads], axis=0)
        all_scaled = jnp.concatenate([only_head(scaled, h) for h in heads], axis=0)
        all_queries = jnp.concatenate([only_head(queries, h) for h in heads], axis=0)
        sums = jnp.concatenate([lse_ref[pl.ds(h, 1), 0:n] for h in heads], axis=1)
        deltas = jnp.concatenate([delta_ref[pl.ds(h, 1), 0:n] for h in heads], axis=1)
        soft = jnp.exp2(nt(keys, all_scaled) - sums)
        back = (soft * (nt(values, ups) - deltas)).astype(BF16)
        dv_ref[part] += nn(soft.astype(BF16), ups)
        dk_ref[part] += nn(back, all_queries)
        for j, h in enumerate(heads):
            rows = pl.ds(pl.multiple_of(h * SIZE, SIZE), SIZE)
            dqt_ref[rows, 0:n] = nn(turned_ref[rows, 0:n], back[:, n * j : n * j + n])
        return carry

    if group == HEADS:
        heads_of(0, 0)
    else:
        lax.fori_loop(0, HEADS // group, heads_of, 0)
    if n < full:
        dq_ref[whole_part] = jnp.zeros((full, HALF), F32)
    dq_ref[part] = dqt_ref[:, 0:n].T * SCALE


def prepare_back(mask, stripes, across, lanes, kern_ref, saved, up_ref, acc, key_ref, query_ref, turned_ref, dv_ref):
    q_ref, k_ref, v_ref = saved
    grid = ACROSS_GRID if across else DOWN_GRID
    key_ref[...] = valid_keys(k_ref[...], mask, stripes)
    query_ref[...] = split_queries(q_ref[...])
    turned = (k_ref[...].astype(F32) * mask).astype(BF16).T
    size = PIXELS // stripes
    for u in range(stripes):
        turned_ref[u] = turned[:, size * u : size * u + size]
    masked = v_ref[...].astype(F32) * mask
    grad = up_ref[...].astype(F32)
    back, kernel_rows, bias_row = position_back(grad.reshape(grid), masked.reshape(grid), kern_ref, lanes, across)
    dv_ref[...] = back.reshape(PIXELS, HALF)
    acc[VEC + 4 : VEC + 14, lanes] += jnp.concatenate([bias_row] + kernel_rows, axis=0)


def finish_back(x_ref, mask, lanes, weight_ref, gain_ref, shift_ref, acc, dq_ref, dk_ref, dv_ref):
    triple = jnp.concatenate([dq_ref[...], dk_ref[...] * (mask * SCALE), dv_ref[...] * mask], axis=1).astype(BF16)
    hat, rstd = normalize(x_ref[...].reshape(PIXELS, DIM).astype(F32))
    normed = (hat * gain_ref[...] + shift_ref[...]).astype(BF16)
    grads = tn(normed, triple)
    for k in range(3):
        acc[0:DIM, DIM * k + lanes.start : DIM * k + lanes.stop] += grads[:, HALF * k : HALF * k + HALF]
    d_normed = nt(triple, weight_ref[...])
    sums = col_sum(triple.astype(F32))
    acc[VEC : VEC + 1, 0:DIM] += col_sum(d_normed * hat)
    acc[VEC + 1 : VEC + 2, 0:DIM] += col_sum(d_normed)
    acc[VEC + 2 : VEC + 3, lanes] += sums[:, 0:HALF]
    acc[VEC + 3 : VEC + 4, lanes] += sums[:, 2 * HALF :]
    return norm_back(d_normed * gain_ref[...], hat, rstd).astype(BF16).reshape(4, PIX, DIM)


def backward_down_kernel(count, first, begin, meta_ref, xd0, xd1, xd2, xd3, dd0, dd1, dd2, dd3,
                         q_in, k_in, v_in, at_in, lse_in, weight_ref, gain_ref, shift_ref, kern_ref,
                         *rest):
    if not begin:
        start, *rest = rest
        *rest, early, sem = rest
    (pd0, pd1, pd2, pd3, acc,
                         x_ref, up_ref, key_ref, query_ref, turned_ref, dq_ref, dk_ref, dv_ref, part_ref,
                         delta_ref, dqt_ref) = rest
    meta = Meta(meta_ref, count)
    step = pl.program_id(0)
    i = first + step
    r, c = meta.row(), meta.col()
    height, width = meta.height(i), meta.width(i)

    @pl.when(step == 0)
    def _():
        if not begin:
            fetch(start, early, sem).start()
        acc[...] = jnp.zeros_like(acc)

    stripe = 4 * c + r
    live = (meta.keep(i) > 0) & (STRIPE * stripe < width)

    @pl.when(live)
    def _():
        mask = down_mask(height, width, stripe).reshape(PIXELS, HALF)
        lanes = slice(HALF, DIM)
        from_rows((xd0, xd1, xd2, xd3), r, x_ref)
        for k, ref in enumerate((dd0, dd1, dd2, dd3)):
            up_ref[pl.ds(pl.multiple_of(lax.rem(r + 4 - k, 4) * PIX, PIX), PIX)] = ref[0]
        prepare_back(mask, 1, False, lanes, kern_ref, (q_in.at[0], k_in.at[0], v_in.at[0]), up_ref, acc,
                     key_ref, query_ref, turned_ref, dv_ref)

        def size(n):
            attend_back(key_ref, query_ref, q_in.at[0], v_in.at[0], turned_ref.at[0], up_ref, at_in.at[0], lse_in.at[0],
                        0, delta_ref, dqt_ref, dq_ref, dk_ref, dv_ref, PIXELS, DOWN_BACK_GROUP, n)

        by_size(down_used(height), DOWN_SIZES, size)
        part_ref[...] = finish_back(x_ref, mask, lanes, weight_ref, gain_ref, shift_ref, acc, dq_ref, dk_ref, dv_ref)
        to_rows((pd0, pd1, pd2, pd3), r, part_ref)

    @pl.when(jnp.logical_not(live))
    def _():
        for ref in (pd0, pd1, pd2, pd3):
            ref[...] = jnp.zeros_like(ref)

    if not begin:

        @pl.when(step == pl.num_programs(0) - 1)
        def _():
            fetch(start, early, sem).wait()
            acc[...] += early[...]


def backward_across_kernel(count, first, begin, last, meta_ref, xa_keep, xa_recv, da_keep, da_recv,
                           q_in, k_in, v_in, at_in, lse_in, weight_ref, gain_ref, shift_ref, kern_ref,
                           *rest):
    if not begin:
        start, *rest = rest
        *rest, early, sem = rest
    if last:
        extra, *rest = rest
    (pa_keep, pa_send, acc_out,
                           acc, x_ref, up_ref, key_ref, query_ref, turned_ref, dq_ref, dk_ref, dv_ref, part_ref,
                           delta_ref, dqt_ref) = rest
    meta = Meta(meta_ref, count)
    step = pl.program_id(0)
    i = first + step
    r, c = meta.row(), meta.col()
    height, width = meta.height(i), meta.width(i)

    @pl.when(step == 0)
    def _():
        if not begin:
            fetch(start, early, sem).start()
        acc[...] = jnp.zeros_like(acc)

    stripe = 4 * r + pair_start(c)
    live = (meta.keep(i) > 0) & (STRIPE * stripe < height)

    @pl.when(live)
    def _():
        mask = across_mask(height, width, stripe).reshape(PIXELS, HALF)
        lanes = slice(0, HALF)
        for u in range(2):
            for xs, ds, side in ((xa_keep, da_keep, c), (xa_recv, da_recv, 1 - c)):
                x_ref[2 * u + side] = xs[0, u]
                up_ref[pl.ds(pl.multiple_of((2 * u + side) * PIX, PIX), PIX)] = ds[0, u]
        prepare_back(mask, 2, True, lanes, kern_ref, (q_in.at[0], k_in.at[0], v_in.at[0]), up_ref, acc,
                     key_ref, query_ref, turned_ref, dv_ref)
        half = PIXELS // 2
        dk_ref[half:] = jnp.zeros((half, HALF), F32)
        dq_ref[half:] = jnp.zeros((half, HALF), F32)

        def stripe_of(u, carry):
            def size(n):
                base = pl.multiple_of(u * half, half)
                attend_back(key_ref, query_ref, q_in.at[0], v_in.at[0], turned_ref.at[u], up_ref,
                            at_in.at[0, u], lse_in.at[0, u], base, delta_ref, dqt_ref, dq_ref, dk_ref, dv_ref,
                            half, HEADS, n)

            by_size(across_used(width), ACROSS_SIZES, size)
            return carry

        lax.fori_loop(0, live_stripes(height, stripe), stripe_of, 0)
        part_ref[...] = finish_back(x_ref, mask, lanes, weight_ref, gain_ref, shift_ref, acc, dq_ref, dk_ref, dv_ref)
        for u in range(2):
            pa_keep[0, u] = part_ref[2 * u + c]
            pa_send[0, u] = part_ref[2 * u + 1 - c]

    @pl.when(jnp.logical_not(live))
    def _():
        pa_keep[...] = jnp.zeros_like(pa_keep)
        pa_send[...] = jnp.zeros_like(pa_send)

    @pl.when(step == pl.num_programs(0) - 1)
    def _():
        if not begin:
            fetch(start, early, sem).wait()
            acc[...] += early[...]
        if last:
            acc_out[:, 0 : 3 * DIM] = acc[0:DIM].astype(BF16)
            vectors = []
            for source, count_rows in ((acc.at[VEC:, 0:DIM], 16), (extra, 8)):
                for k in range(count_rows):
                    vectors += [source[k : k + 1, 0:HALF], source[k : k + 1, HALF:DIM]]
            vectors.append(jnp.zeros((DIM - 48, HALF), F32))
            acc_out[:, 3 * DIM :] = jnp.concatenate(vectors, axis=0).astype(BF16)
        else:
            acc_out[...] = acc[...]


def finish_kernel(count, first, meta_ref, dm_ref, pd0, pd1, pd2, pd3, pa_keep, pa_recv, out_ref, total, wide):
    meta = Meta(meta_ref, count)
    r, c = meta.row(), meta.col()
    total[...] = dm_ref[0].astype(F32).reshape(4, ROWS, SLOT, DIM)
    for k, ref in enumerate((pd0, pd1, pd2, pd3)):
        total[lax.rem(r + 4 - k, 4)] += ref[0].astype(F32).reshape(ROWS, SLOT, DIM)
    for where, ref in own_stripes(pa_keep, pa_recv, c):
        total[:, where] += ref[...].astype(F32).reshape(4, STRIPE, SLOT, DIM)
    out_ref[0] = merge_cols(total, wide).astype(BF16)


def whole(shape):
    zeros = (0,) * len(shape)
    return pl.BlockSpec(shape, lambda i, *unused: zeros)


def per_image(shape, first=0):
    zeros = (0,) * len(shape)
    return pl.BlockSpec((1,) + shape, lambda i, *unused: (first + i,) + zeros)


def call(body, name, batch, scalars, inputs, outputs, scratch, micros, held=None, waits=()):
    in_specs = [spec for spec, unused in inputs]
    out_specs = [spec for spec, unused in outputs]
    moved = sum(value.size * value.dtype.itemsize for unused, value in inputs)
    aliases = {}
    held = held or {}
    inner, skipped, extra = body, len(scalars) + len(inputs), len(held) + len(waits)

    def body(*refs):
        inner(*refs[:skipped], *refs[skipped + extra :])

    for k, place in enumerate(held):
        aliases[skipped + k] = place
    in_specs = in_specs + [pl.BlockSpec(memory_space=pl.ANY)] * extra
    inputs = inputs + [(None, value) for value in list(held.values()) + list(waits)]
    return list(pl.pallas_call(
        body,
        out_shape=[shape for unused, shape in outputs],
        grid_spec=pltpu.PrefetchScalarGridSpec(
            num_scalar_prefetch=len(scalars),
            grid=(batch,),
            in_specs=in_specs,
            out_specs=out_specs,
            scratch_shapes=scratch,
        ),
        compiler_params=pltpu.CompilerParams(
            dimension_semantics=("arbitrary",), vmem_limit_bytes=VMEM_LIMIT
        ),
        input_output_aliases=aliases,
        cost_estimate=pl.CostEstimate(flops=micros * 10**9, bytes_accessed=moved, transcendentals=0),
        name=name,
    )(*scalars, *[value for unused, value in inputs]))


def struct(shape, dtype):
    return jax.ShapeDtypeStruct(shape, dtype)


def images_out(batch, shape, dtype):
    return per_image(shape), struct((batch,) + shape, dtype)


def whole_out(shape, dtype=F32):
    return whole(shape), struct(shape, dtype)


def row_exchange(parts):
    size = lax.axis_size("row")
    return [parts[0]] + [
        lax.ppermute(parts[k], "row", [(q, (q + k) % size) for q in range(size)]) for k in range(1, size)
    ]


def col_exchange(keep, send):
    return [keep, lax.ppermute(send, "col", [(0, 1), (1, 0)])]


def together(*values):
    return lax.optimization_barrier(values)


def bits_of(size):
    found = []
    bit = 1
    while bit < size:
        found.append(bit)
        bit *= 2
    return found


def kept_total(flags):
    total = flags
    size = lax.axis_size("batch")
    for bit in bits_of(size):
        total = total + lax.ppermute(total, "batch", [(q, q ^ bit) for q in range(size)])
    return total


ALL = ("batch", "row", "col")
NEAR = ("batch", "col")


def send_shares(rows, axes):
    places = lax.axis_size(axes)
    sent = rows.astype(BF16).reshape((places, -1) + rows.shape[1:])
    return lax.all_to_all(sent, axes, 0, 0)


def sum_shares(received):
    return jnp.sum(received.astype(F32), axis=0).astype(BF16)


def spread_share(share, axes):
    return jnp.broadcast_to(share[None], (lax.axis_size(axes),) + share.shape)


def gather_spread(sent, axes):
    return lax.all_to_all(sent, axes, 0, 0).reshape((-1,) + sent.shape[2:])


def send_rows(share):
    size = lax.axis_size("row")
    return [lax.ppermute(share, "row", [(q, (q + k) % size) for q in range(size)]) for k in range(1, size)]


def per_device(batch, devices, tokens, heights, widths, keep_flags, out_grad, first_gain, first_shift, triple_weight,
               query_value_bias, position_kernel, position_bias, mixing_weight, mixing_bias, second_gain, second_shift,
               expand_weight, expand_bias, reduce_weight, reduce_bias):
    count = tokens.shape[0]
    chunks = count // batch
    r, c = lax.axis_index("row"), lax.axis_index("col")
    meta = jnp.concatenate(
        [heights, widths, keep_flags[:, 0], keep_flags[:, 1], jnp.stack([r, c]).astype(jnp.int32)]
    )
    def full(value):
        return whole(value.shape), value

    def chunk_in(value):
        return per_image(value.shape[1:]), value

    def grid_out(first):
        return per_image((ROWS, ROWS, DIM), first), struct((count, ROWS, ROWS, DIM), BF16)

    pix = (PIX, DIM)
    half = (PIX, HALF)
    pair = (2, PIX, DIM)
    pair_half = (2, PIX, HALF)

    def all_images(shape, dtype, first):
        return per_image(shape, first), struct((count,) + shape, dtype)

    blocks = pltpu.VMEM((4, PIX, DIM), BF16)
    low = pltpu.VMEM((PIXELS, HALF), BF16)
    high = pltpu.VMEM((PIXELS, HALF), F32)
    pairs = pltpu.VMEM((PIXELS, DIM), BF16)
    low_blocks = pltpu.VMEM((4, PIX, HALF), BF16)
    parts_high = pltpu.VMEM((4, ROWS, SLOT, DIM), F32)
    wide = pltpu.VMEM((ROWS, 32, DIM), F32)

    def prepare(k, waits):
        first = k * batch
        outs = call(
            functools.partial(prep_kernel, count, first), "prep", batch, [meta],
            [(per_image((ROWS, ROWS, DIM), first), tokens)],
            [images_out(batch, pix, BF16)] * 4 + [images_out(batch, pair, BF16)] * 2,
            [wide, parts_high], 2 * batch, {}, waits)
        return outs[0:4], outs[4:6]

    flat = (PIXELS, HALF)
    save_scratch = [pltpu.VMEM((3, PIXELS, HALF), BF16), pltpu.SemaphoreType.DMA((3,))]

    def across_forward(k, taken, held, waits):
        first = k * batch
        shapes = [(pair_half, BF16)] * 2 + [(flat, BF16)] * 3 + [((2, HALF, PIXELS // 2), BF16), ((2, 8, PIXELS // 2), F32)]
        return call(
            functools.partial(forward_across_kernel, count, first), "across_forward", batch, [meta],
            [chunk_in(v) for v in taken] + [full(v) for v in (wa, ba, gain1, shift1, kern, pos)],
            [
                (pl.BlockSpec(memory_space=pl.ANY) if 2 <= k < 5 else per_image(shape, first), struct((count,) + shape, dtype))
                for k, (shape, dtype) in enumerate(shapes)
            ],
            [blocks, low, pairs, pltpu.VMEM((2, HEADS, SIZE + 16, PIXELS // 2), BF16), high, low_blocks,
             pltpu.VMEM((HALF, PIXELS // 2), F32)] + save_scratch,
            5 * batch, dict(enumerate(held)), waits)

    def down_forward(k, taken, waits):
        first = k * batch
        out = pl.BlockSpec(memory_space=pl.ANY), struct((batch,) + flat, BF16)
        outs = call(
            functools.partial(forward_down_kernel, count, first), "down_forward", batch, [meta],
            [chunk_in(v) for v in taken] + [full(v) for v in (wd, bd, gain1, shift1, kern, pos)],
            [images_out(batch, half, BF16)] * 4
            + [out, out, out, images_out(batch, (HALF, PIXELS), BF16), images_out(batch, (8, PIXELS), F32)],
            [blocks, low, pairs, pltpu.VMEM((1, HEADS, SIZE + 16, PIXELS), BF16), high, low_blocks,
             pltpu.VMEM((HALF, PIXELS), F32)] + save_scratch,
            6 * batch, {}, waits)
        return outs[0:4], outs[4:]

    own0, sent0 = prepare(0, [])
    own0, keep_flags, triple_weight, query_value_bias, position_kernel = together(
        own0, keep_flags, triple_weight, query_value_bias, position_kernel
    )
    kept = kept_total(jnp.sum(keep_flags.astype(F32), axis=0))
    share = kept / (count * lax.axis_size("batch"))
    factors = (keep_flags.astype(F32) / share).reshape(-1)

    def branch_weight(lo):
        return jnp.concatenate([triple_weight[:, DIM * k + lo : DIM * k + lo + HALF] for k in range(3)], axis=1)

    wa, wd = branch_weight(0), branch_weight(HALF)
    zeros = jnp.zeros((HALF,), F32)
    ba = jnp.concatenate([query_value_bias[0, :HALF], zeros, query_value_bias[1, :HALF]])[None]
    bd = jnp.concatenate([query_value_bias[0, HALF:], zeros, query_value_bias[1, HALF:]])[None]
    gain1, shift1 = first_gain[None], first_shift[None]
    gain2, shift2 = second_gain[None], second_shift[None]
    kern = jnp.pad(position_kernel.reshape(9, DIM), ((0, 7), (0, 0)))
    pos = position_bias[None]

    col0 = col_exchange(*sent0)
    row0 = row_exchange(own0)
    own1, sent1 = prepare(1, [factors])
    across0 = across_forward(0, col0, [], own1[0:1])
    own1, sent1, across_done = together(own1, sent1, across0[0])
    across0[0] = across_done
    col1 = col_exchange(*sent1)
    row1 = row_exchange(own1)
    joined0, saved0 = down_forward(0, row0, across0[0:1])
    across1 = across_forward(1, col1, across0, saved0[0:1])
    joined_across = col_exchange(*across1[0:2])
    joined1, saved1 = down_forward(1, row1, across1[2:3])
    row_joined0 = row_exchange(joined0)
    row_joined1 = row_exchange(joined1)

    def middle(k, own, row_joined, held, sums, waits):
        first = k * batch
        acc_shape = (DIM, 2 * HIDDEN + DIM)
        return call(
            functools.partial(middle_kernel, count, first), "middle", batch, [meta, factors],
            [chunk_in(v) for v in own + row_joined]
            + [(per_image(v.shape[1:], first), v) for v in joined_across + [out_grad]]
            + [full(v) for v in (mixing_weight, mixing_bias[None], gain2, shift2, expand_weight, expand_bias[None],
                                 reduce_weight, reduce_bias[None])]
            + ([(pl.BlockSpec(memory_space=pl.ANY), sums[0]), full(sums[1])] if sums else []),
            [all_images((ROWS, ROWS, DIM), BF16, first), all_images((4,) + pix, BF16, first)]
            + [images_out(batch, half, BF16)] * 4 + [images_out(batch, pair_half, BF16)] * 2
            + [whole_out(acc_shape, BF16), whole_out((8, DIM))],
            [pltpu.VMEM(acc_shape, F32), pltpu.VMEM((4,) + pix, BF16), parts_high,
             pltpu.VMEM((4, ROWS, SLOT, HALF), F32), pltpu.VMEM((4,) + pix, BF16), parts_high, parts_high, wide]
            + ([pltpu.VMEM(acc_shape, BF16), pltpu.SemaphoreType.DMA] if sums else []),
            8 * batch, held, waits)

    mid0 = middle(0, own0, row_joined0, {}, [], saved1[0:1])
    row_grad0 = row_exchange(mid0[2:6])
    col_grad0 = col_exchange(*mid0[6:8])
    mid1 = middle(1, own1, row_joined1, {0: mid0[0], 1: mid0[1]}, mid0[8:10], [])
    output, middles = mid1[0:2]
    feed, row_grad0, col_grad0 = together(mid1[8], row_grad0, col_grad0)
    row_grad1 = row_exchange(mid1[2:6])
    col_grad1 = col_exchange(*mid1[6:8])
    received = send_shares(feed, NEAR)

    back_scratch = [high, high, high, blocks, pltpu.VMEM((8, PIXELS), F32), pltpu.VMEM((HALF, PIXELS), F32)]
    back_shape = (VEC + 16, 3 * DIM)

    def early_scratch(sums):
        return [pltpu.VMEM(back_shape, F32), pltpu.SemaphoreType.DMA] if sums else []

    def down_backward(k, taken, row_grad, saved, sums, waits):
        first = k * batch
        outs = call(
            functools.partial(backward_down_kernel, count, first, not sums), "down_backward", batch, [meta],
            [chunk_in(v) for v in taken + row_grad + saved] + [full(v) for v in (wd, gain1, shift1, kern)]
            + [(pl.BlockSpec(memory_space=pl.ANY), v) for v in sums],
            [images_out(batch, pix, BF16)] * 4 + [whole_out(back_shape)],
            [blocks, low, low, pairs, pltpu.VMEM((1, HALF, PIXELS), BF16)] + back_scratch + early_scratch(sums),
            11 * batch, {}, waits)
        return outs[0:4], outs[4:]

    def across_backward(k, taken, col_grad, sums, waits):
        first = k * batch
        last = k == chunks - 1
        out = whole_out((DIM, PACKED), BF16) if last else whole_out(back_shape)
        outs = call(
            functools.partial(backward_across_kernel, count, first, not sums, last), "across_backward", batch, [meta],
            [chunk_in(v) for v in taken + col_grad] + [(per_image(v.shape[1:], first), v) for v in across1[2:]]
            + [full(v) for v in (wa, gain1, shift1, kern)]
            + [(pl.BlockSpec(memory_space=pl.ANY), v) for v in sums[:1]] + [full(v) for v in sums[1:]],
            [images_out(batch, pair, BF16)] * 2 + [out],
            [pltpu.VMEM(back_shape, F32), blocks, low, low, pairs, pltpu.VMEM((2, HALF, PIXELS // 2), BF16)]
            + back_scratch + early_scratch(sums), 9 * batch, {}, waits)
        return outs[0:2], outs[2]

    part0, sums = across_backward(0, col0, col_grad0, [], mid1[8:9] + row_grad0[1:])
    col_part0 = col_exchange(*part0)
    received, sums, row_grad1, col_grad1 = together(received, sums, row_grad1, col_grad1)
    share = sum_shares(received)
    others = send_rows(share)
    part0, sums = down_backward(0, row0, row_grad0, saved0, [sums], row_grad1[1:] + col_grad1[1:])
    row_part0 = row_exchange(part0)
    others, sums, col_part0 = together(others, sums, col_part0)
    feed = gather_spread(spread_share(sum_shares(jnp.stack([share] + others)), NEAR), NEAR)
    part1, sums = down_backward(1, row1, row_grad1, saved1, sums, col_part0[1:])
    row_part1 = row_exchange(part1)
    feed, sums = together(feed, sums)
    part1, back = across_backward(1, col1, col_grad1, sums + [mid1[9]], row_part0[1:])
    col_part1 = col_exchange(*part1)
    back, row_part1, col_part0 = together(back, row_part1, col_part0)
    received = send_shares(back, ALL)

    def finish(k, row_part, col_part, held, waits):
        first = k * batch
        return call(
            functools.partial(finish_kernel, count, first), "finish", batch, [meta],
            [(per_image(middles.shape[1:], first), middles)] + [chunk_in(v) for v in row_part + col_part],
            [grid_out(first)], [parts_high, wide], 2 * batch, held, waits)

    feed = feed.astype(F32)
    feed = [feed[:, 0:HIDDEN].T, feed[:, HIDDEN : 2 * HIDDEN], feed[:, 2 * HIDDEN :]]
    grad0 = finish(0, row_part0, col_part0, {}, [back])
    sent = spread_share(sum_shares(received), ALL)
    sent, feed, grad0, col_part1 = together(sent, feed, grad0, col_part1)
    rows = gather_spread(sent, ALL)
    tokens_grad = finish(1, row_part1, col_part1, {0: grad0[0]}, [])[0]
    back_rows = rows.astype(F32)

    triple_weight_grad = back_rows[:, 0 : 3 * DIM]
    vectors = back_rows[0:48, 3 * DIM :].reshape(24, DIM)
    rows = vectors[16:24]
    return (
        output,
        tokens_grad,
        vectors[0],
        vectors[1],
        triple_weight_grad,
        vectors[2:4],
        vectors[5:14].reshape(3, 3, DIM),
        vectors[4],
        feed[2],
        rows[7],
        rows[5],
        rows[6],
        feed[1],
        rows[0:4].reshape(HIDDEN),
        feed[0],
        rows[4],
    )


def solution(mesh):
    spread = P("batch", "row", "col", None)
    in_specs = (spread, P("batch"), P("batch"), P("batch", None), spread) + (P(),) * 14
    out_specs = (spread, spread) + (P(),) * 14
    devices = mesh.shape["batch"] * mesh.shape["row"] * mesh.shape["col"]
    return jax.shard_map(
        functools.partial(per_device, 2, devices),
        mesh=mesh, in_specs=in_specs, out_specs=out_specs, check_vma=False)
```

profile of v0, /device:TPU:0, one launch (start us, length us, event | category | flops | bytes accessed | tf_op | source)
XLA Modules:
  0.0 265.1 jit_solution(5342856712870628872)
XLA Ops:
  1.4 3.1 %copy.54.refs_1_ = bf16[4,28,28,256]{3,2,1,0:T(8,128)(2,1)} copy(bf16[4,28,28,256]{3,0,2,1:T(4,128)(2,1)} %param.19) | data formatting | bytes 3211264 | tf_op args[0]
  5.1 3.3 %prep.2 = (bf16[2,224,256]{2,1,0:T(8,128)(2,1)}, bf16[2,224,256]{2,1,0:T(8,128)(2,1)}, bf16[2,224,256]{2,1,0:T(8,128)(2,1)}, bf16[2,224,256]{2,1,0:T(8,128)(2,1)...) custom-call(s32[18]{0:T(128)} %concatenate.15.refs_0_, bf16[4,28,28,256]{3,2,1,0:T(8,128)(2,1)} %copy.54.refs_1_), custom_call_target="tpu_custom_call" | custom-call | flops 4000000000 | bytes 1605632 | tf_op jit(solution)/shard_map/prep/pallas_call | solution.py:797
  9.0 2.6 collective-permute-start.7
  11.7 2.6 collective-permute-start.8
  26.3 3.2 %prep.3 = (bf16[2,224,256]{2,1,0:T(8,128)(2,1)}, bf16[2,224,256]{2,1,0:T(8,128)(2,1)}, bf16[2,224,256]{2,1,0:T(8,128)(2,1)}, bf16[2,224,256]{2,1,0:T(8,128)(2,1)...) custom-call(s32[18]{0:T(128)} %concatenate.15.refs_0_, bf16[4,28,28,256]{3,2,1,0:T(8,128)(2,1)} %copy.54.refs_1_, ...), custom_call_target="tpu_custom_call" | custom-call | flops 4000000000 | bytes 1605632 | tf_op jit(solution)/shard_map/prep/pallas_call | solution.py:797
  30.2 7.1 %across_forward.2 = (bf16[4,2,224,128]{3,2,1,0:T(8,128)(2,1)}, bf16[4,2,224,128]{3,2,1,0:T(8,128)(2,1)}, bf16[4,896,128]{2,1,0:T(8,128)(2,1)}, bf16[4,896,128]{2...) custom-call(s32[18]{0:T(128)} %concatenate.15.refs_0_, ...), custom_call_target="tpu_custom_call" | custom-call | flops 10000000000 | bytes 1135104 | tf_op jit(solution)/shard_map/across_forward/pallas_call | solution.py:797
  38.4 3.1 %collective-permute-start.5 = (bf16[2,224,256]{2,1,0:T(8,128)(2,1)S(1)}, bf16[2,224,256]{2,1,0:T(8,128)(2,1)S(1)}, u32[]{:S(2)}, u32[]{:S(2)}) collective-permute-start(bf16[2,224,256]{2,1,0:T(8,128)(2,1)S(1)} %copy-done.21), channel_id=1, source_target_pairs={{0,6},{2,0},{4,2},{6,4},{1,7},{3,1},{5,3},{7,5},{8,14},{10,8},{12,... | collective-permute-start | bytes 688136 | tf_op jit(solution)/shard_map/ppermute | solution.py:831
  42.9 8.5 %down_forward.2 = (bf16[2,224,128]{2,1,0:T(8,128)(2,1)}, bf16[2,224,128]{2,1,0:T(8,128)(2,1)}, bf16[2,224,128]{2,1,0:T(8,128)(2,1)}, bf16[2,224,128]{2,1,0:T(8,1...) custom-call(s32[18]{0:T(128)} %concatenate.15.refs_0_, ...), custom_call_target="tpu_custom_call" | custom-call | flops 12000000000 | bytes 1135104 | tf_op jit(solution)/shard_map/down_forward/pallas_call | solution.py:797
  53.5 3.1 %across_forward.3 = (bf16[4,2,224,128]{3,2,1,0:T(8,128)(2,1)}, bf16[4,2,224,128]{3,2,1,0:T(8,128)(2,1)}, bf16[4,896,128]{2,1,0:T(8,128)(2,1)}, bf16[4,896,128]{2...) custom-call(s32[18]{0:T(128)} %concatenate.15.refs_0_, ...), custom_call_target="tpu_custom_call", output_to_operand_aliasing={{0}: (9, {}), {1}: (10, {}), {2}: (11, {}), {3}: (12, {}), ... | custom-call | flops 10000000000 | bytes 1135104 | tf_op jit(solution)/shard_map/across_forward/pallas_call | solution.py:797
  56.7 3.1 %collective-permute-start.16 = (bf16[2,224,128]{2,1,0:T(8,128)(2,1)S(1)}, bf16[2,224,128]{2,1,0:T(8,128)(2,1)S(1)}, u32[]{:S(2)}, u32[]{:S(2)}) collective-permute-start(bf16[2,224,128]{2,1,0:T(8,128)(2,1)S(1)} %copy-done.39), channel_id=1, source_target_pairs={{0,6},{2,0},{4,2},{6,4},{1,7},{3,1},{5,3},{7,5},{8,14},{10,8},{12,... | collective-permute-start | bytes 344072 | tf_op jit(solution)/shard_map/ppermute | solution.py:831
  61.9 3.1 %down_forward.3 = (bf16[2,224,128]{2,1,0:T(8,128)(2,1)}, bf16[2,224,128]{2,1,0:T(8,128)(2,1)}, bf16[2,224,128]{2,1,0:T(8,128)(2,1)}, bf16[2,224,128]{2,1,0:T(8,1...) custom-call(s32[18]{0:T(128)} %concatenate.15.refs_0_, ...), custom_call_target="tpu_custom_call" | custom-call | flops 12000000000 | bytes 1135104 | tf_op jit(solution)/shard_map/down_forward/pallas_call | solution.py:797
  70.3 15.0 %middle.2 = (bf16[4,28,28,256]{3,2,1,0:T(8,128)(2,1)}, bf16[4,4,224,256]{3,2,1,0:T(8,128)(2,1)}, bf16[2,224,128]{2,1,0:T(8,128)(2,1)}, bf16[2,224,128]{2,1,0:T(8...) custom-call(s32[18]{0:T(128)} %concatenate.15.refs_0_, ...), custom_call_target="tpu_custom_call" | custom-call | flops 16000000000 | bytes 5087232 | tf_op jit(solution)/shard_map/middle/pallas_call | solution.py:797
  91.5 15.1 %middle.3 = (bf16[4,28,28,256]{3,2,1,0:T(8,128)(2,1)}, bf16[4,4,224,256]{3,2,1,0:T(8,128)(2,1)}, bf16[2,224,128]{2,1,0:T(8,128)(2,1)}, bf16[2,224,128]{2,1,0:T(8...) custom-call(s32[18]{0:T(128)} %concatenate.15.refs_0_, ...), custom_call_target="tpu_custom_call", output_to_operand_aliasing={{0}: (23, {}), {1}: (24, {})} | custom-call | flops 16000000000 | bytes 6275072 | tf_op jit(solution)/shard_map/middle/pallas_call | solution.py:797
  108.0 2.6 collective-permute-start.23
  112.1 14.5 %all-to-all-start = ((bf16[8,32,2304]{2,1,0:T(8,128)(2,1)}), bf16[8,32,2304]{2,1,0:T(8,128)(2,1)S(1)}, u32[]{:S(2)}, u32[]{:S(2)}) async-start(bf16[8,32,2304]{2,1,0:T(8,128)(2,1)} %bitcast.49), calls=%async_computation | async-start | bytes 2359296 | tf_op jit(solution)/shard_map/all_to_all | solution.py:867
  126.6 11.1 %across_backward.2 = (bf16[2,2,224,256]{3,2,1,0:T(8,128)(2,1)}, bf16[2,2,224,256]{3,2,1,0:T(8,128)(2,1)}, f32[272,768]{1,0:T(8,128)}) custom-call(s32[18]{0:T(128)} %concatenate.15.refs_0_, bf16[2,2,224,256]{3,2,1,0:T(8,128)(2,1)} %get-tuple-element.159.refs_1_, bf16[2,2,224,256]{3,2,1,0:T(8,128)(2,1)} %copy-done.8, ...), custom_call_target="tpu_custom_call" | custom-call | flops 17999998976 | bytes 5376000 | tf_op jit(solution)/shard_map/across_backward/pallas_call | solution.py:797
  139.9 2.6 all-to-all-done
  146.2 15.3 %down_backward.2 = (bf16[2,224,256]{2,1,0:T(8,128)(2,1)}, bf16[2,224,256]{2,1,0:T(8,128)(2,1)}, bf16[2,224,256]{2,1,0:T(8,128)(2,1)}, bf16[2,224,256]{2,1,0:T(8,128)(2,1)}, f32[272,768]{1,0:T(8,128)}) custom-call(s32[18]{0:T(128)} %concatenate.15.refs_0_, bf16[2,224,256]{2,1,0:T(8,128)(2,1)} %get-tuple-element.178.refs_1_.refs_2_, ...), custom_call_target="tpu_custom_call" | custom-call | flops 22000001024 | bytes 4319232 | tf_op jit(solution)/shard_map/down_backward/pallas_call | solution.py:797
  162.0 2.3 collective-permute-start.30
  167.1 3.6 %all-to-all-start.1 = ((bf16[8,32,2304]{2,1,0:T(8,128)(2,1)}), bf16[8,32,2304]{2,1,0:T(8,128)(2,1)S(1)}, u32[]{:S(2)}, u32[]{:S(2)}) async-start(bf16[8,32,2304]{2,1,0:T(8,128)(2,1)} %broadcast_in_dim.60), calls=%async_computation.1 | async-start | bytes 2359296 | tf_op jit(solution)/shard_map/all_to_all | solution.py:879
  170.7 7.0 %down_backward.3 = (bf16[2,224,256]{2,1,0:T(8,128)(2,1)}, bf16[2,224,256]{2,1,0:T(8,128)(2,1)}, bf16[2,224,256]{2,1,0:T(8,128)(2,1)}, bf16[2,224,256]{2,1,0:T(8,128)(2,1)}, f32[272,768]{1,0:T(8,128)}) custom-call(s32[18]{0:T(128)} %concatenate.15.refs_0_, bf16[2,224,256]{2,1,0:T(8,128)(2,1)} %get-tuple-element.165.refs_9_.refs_1_.refs_2_, ...), custom_call_target="tpu_custom_call" | custom-call | flops 22000001024 | bytes 4319232 | tf_op jit(solution)/shard_map/down_backward/pallas_call | solution.py:797
  179.3 7.3 %all-to-all-done.1 = bf16[8,32,2304]{2,1,0:T(8,128)(2,1)S(1)} async-done(((bf16[8,32,2304]{2,1,0:T(8,128)(2,1)}), bf16[8,32,2304]{2,1,0:T(8,128)(2,1)S(1)}, u32[]{:S(2)}, u32[]{:S(2)}) %all-to-all-start.1) | async-done | bytes 1179680 | tf_op jit(solution)/shard_map/all_to_all | solution.py:879
  187.8 5.0 %across_backward.3 = (bf16[2,2,224,256]{3,2,1,0:T(8,128)(2,1)}, bf16[2,2,224,256]{3,2,1,0:T(8,128)(2,1)}, bf16[256,896]{1,0:T(8,128)(2,1)}) custom-call(s32[18]{0:T(128)} %concatenate.15.refs_0_, bf16[2,2,224,256]{3,2,1,0:T(8,128)(2,1)} %get-tuple-element.169.refs_1_, bf16[2,2,224,256]{3,2,1,0:T(8,128)(2,1)} %copy-done.7, ...), custom_call_target="tpu_custom_call" | custom-call | flops 17999998976 | bytes 6219776 | tf_op jit(solution)/shard_map/across_backward/pallas_call | solution.py:797
  192.8 5.8 %collective-permute-done.34.refs_5_ = bf16[2,224,256]{2,1,0:T(8,128)(2,1)S(1)} collective-permute-done((bf16[2,224,256]{2,1,0:T(8,128)(2,1)}, bf16[2,224,256]{2,1,0:T(8,128)(2,1)S(1)}, u32[]{:S(2)}, u32[]{:S(2)}) %collective-permute-start.34) | collective-permute-done | bytes 229408 | tf_op jit(solution)/shard_map/ppermute | solution.py:831
  199.3 23.9 %all-to-all-start.2 = ((bf16[32,8,896]{2,1,0:T(8,128)(2,1)}), bf16[32,8,896]{2,1,0:T(8,128)(2,1)S(1)}, u32[]{:S(2)}, u32[]{:S(2)}) async-start(bf16[32,8,896]{2,1,0:T(8,128)(2,1)} %bitcast.50), calls=%async_computation.2 | async-start | bytes 917504 | tf_op jit(solution)/shard_map/all_to_all | solution.py:867
  227.1 3.6 %finish.2.refs_8_ = bf16[4,28,28,256]{3,2,1,0:T(8,128)(2,1)} custom-call(s32[18]{0:T(128)} %concatenate.15.refs_0_, bf16[4,4,224,256]{3,2,1,0:T(8,128)(2,1)} %get-tuple-element.200.refs_1_, bf16[2,224,256]{2,1,0:T(8,128)(2,1)} %get-tuple-element.268.refs_2_, bf16[2,224,256]{2,1,0:T(8,128)(2,1)} %copy-done.23, bf16[2,224,256]{2,1,0:T(8,128)(2,1)} %copy-done.24, ...), custom_call_target="tpu_custom_call" | custom-call | flops 4000000000 | bytes 3670016 | tf_op jit(solution)/shard_map/finish/pallas_call | solution.py:797
  230.8 7.4 %all-to-all-done.2 = bf16[32,8,896]{2,1,0:T(8,128)(2,1)S(1)} async-done(((bf16[32,8,896]{2,1,0:T(8,128)(2,1)}), bf16[32,8,896]{2,1,0:T(8,128)(2,1)S(1)}, u32[]{:S(2)}, u32[]{:S(2)}) %all-to-all-start.2) | async-done | bytes 458784 | tf_op jit(solution)/shard_map/all_to_all | solution.py:867
  238.2 2.6 collective-permute-done.35.refs_7_
  241.7 4.8 %all-to-all-start.3 = ((bf16[32,8,896]{2,1,0:T(8,128)(2,1)}), bf16[32,8,896]{2,1,0:T(8,128)(2,1)S(1)}, u32[]{:S(2)}, u32[]{:S(2)}) async-start(bf16[32,8,896]{2,1,0:T(8,128)(2,1)} %broadcast_in_dim.61), calls=%async_computation.3 | async-start | bytes 917504 | tf_op jit(solution)/shard_map/all_to_all | solution.py:879
  246.5 4.1 %copy.59 = bf16[4,28,28,256]{3,0,2,1:T(4,128)(2,1)} copy(bf16[4,28,28,256]{3,2,1,0:T(8,128)(2,1)} %get-tuple-element.296) | data formatting | bytes 3211264
  250.7 3.6 %finish.3 = bf16[4,28,28,256]{3,2,1,0:T(8,128)(2,1)} custom-call(s32[18]{0:T(128)} %concatenate.15.refs_0_, bf16[4,4,224,256]{3,2,1,0:T(8,128)(2,1)} %get-tuple-element.200.refs_1_, bf16[2,224,256]{2,1,0:T(8,128)(2,1)} %get-tuple-element.262.refs_2_, bf16[2,224,256]{2,1,0:T(8,128)(2,1)} %copy-done.26, ...), custom_call_target="tpu_custom_call", output_to_operand_aliasing={{}: (8, {})} | custom-call | flops 4000000000 | bytes 3670016 | tf_op jit(solution)/shard_map/finish/pallas_call | solution.py:797
  254.3 4.1 %copy.60 = bf16[4,28,28,256]{3,0,2,1:T(4,128)(2,1)} copy(bf16[4,28,28,256]{3,2,1,0:T(8,128)(2,1)} %finish.3) | data formatting | bytes 3211264
  (188 shorter events, 59.8 us)
Async XLA Ops:
  9.0 29.4 %collective-permute-start.7 = (bf16[2,224,256]{2,1,0:T(8,128)(2,1)}, bf16[2,224,256]{2,1,0:T(8,128)(2,1)S(1)}, u32[]{:S(2)}, u32[]{:S(2)}) collective-permute-start(bf16[2,224,256]{2,1,0:T(8,128)(2,1)} %get-tuple-element.179.refs_3_), channel_id=1, source_target_pairs={{0,2},{2,4},{4,6},{6,0},{1,3},{3,5},{5,7},{7,1},{8,10},{10,12},{12... | collective-permute-start | bytes 688136 | tf_op jit(solution)/shard_map/ppermute | solution.py:831
  11.7 29.8 %collective-permute-start.8 = (bf16[2,224,256]{2,1,0:T(8,128)(2,1)}, bf16[2,224,256]{2,1,0:T(8,128)(2,1)S(1)}, u32[]{:S(2)}, u32[]{:S(2)}) collective-permute-start(bf16[2,224,256]{2,1,0:T(8,128)(2,1)} %get-tuple-element.180.refs_4_), channel_id=1, source_target_pairs={{0,4},{2,6},{4,0},{6,2},{1,5},{3,7},{5,1},{7,3},{8,12},{10,14},{12... | collective-permute-start | bytes 688136 | tf_op jit(solution)/shard_map/ppermute | solution.py:831
  14.3 27.8 %collective-permute-start.9 = (bf16[2,224,256]{2,1,0:T(8,128)(2,1)}, bf16[2,224,256]{2,1,0:T(8,128)(2,1)S(1)}, u32[]{:S(2)}, u32[]{:S(2)}) collective-permute-start(bf16[2,224,256]{2,1,0:T(8,128)(2,1)} %get-tuple-element.181.refs_5_), channel_id=1, source_target_pairs={{0,6},{2,0},{4,2},{6,4},{1,7},{3,1},{5,3},{7,5},{8,14},{10,8},{12,... | collective-permute-start | bytes 688136 | tf_op jit(solution)/shard_map/ppermute | solution.py:831
  37.3 19.3 %collective-permute-start.3 = (bf16[2,224,256]{2,1,0:T(8,128)(2,1)S(1)}, bf16[2,224,256]{2,1,0:T(8,128)(2,1)S(1)}, u32[]{:S(2)}, u32[]{:S(2)}) collective-permute-start(bf16[2,224,256]{2,1,0:T(8,128)(2,1)S(1)} %copy-done.19), channel_id=1, source_target_pairs={{0,2},{2,4},{4,6},{6,0},{1,3},{3,5},{5,7},{7,1},{8,10},{10,12},{12... | collective-permute-start | bytes 688136 | tf_op jit(solution)/shard_map/ppermute | solution.py:831
  38.1 21.7 %collective-permute-start.4 = (bf16[2,224,256]{2,1,0:T(8,128)(2,1)S(1)}, bf16[2,224,256]{2,1,0:T(8,128)(2,1)S(1)}, u32[]{:S(2)}, u32[]{:S(2)}) collective-permute-start(bf16[2,224,256]{2,1,0:T(8,128)(2,1)S(1)} %copy-done.20), channel_id=1, source_target_pairs={{0,4},{2,6},{4,0},{6,2},{1,5},{3,7},{5,1},{7,3},{8,12},{10,14},{12... | collective-permute-start | bytes 688136 | tf_op jit(solution)/shard_map/ppermute | solution.py:831
  38.4 22.8 %collective-permute-start.5 = (bf16[2,224,256]{2,1,0:T(8,128)(2,1)S(1)}, bf16[2,224,256]{2,1,0:T(8,128)(2,1)S(1)}, u32[]{:S(2)}, u32[]{:S(2)}) collective-permute-start(bf16[2,224,256]{2,1,0:T(8,128)(2,1)S(1)} %copy-done.21), channel_id=1, source_target_pairs={{0,6},{2,0},{4,2},{6,4},{1,7},{3,1},{5,3},{7,5},{8,14},{10,8},{12,... | collective-permute-start | bytes 688136 | tf_op jit(solution)/shard_map/ppermute | solution.py:831
  51.4 15.2 %collective-permute-start.14 = (bf16[2,224,128]{2,1,0:T(8,128)(2,1)}, bf16[2,224,128]{2,1,0:T(8,128)(2,1)S(1)}, u32[]{:S(2)}, u32[]{:S(2)}) collective-permute-start(bf16[2,224,128]{2,1,0:T(8,128)(2,1)} %get-tuple-element.191), channel_id=1, source_target_pairs={{0,2},{2,4},{4,6},{6,0},{1,3},{3,5},{5,7},{7,1},{8,10},{10,12},{12... | collective-permute-start | bytes 344072 | tf_op jit(solution)/shard_map/ppermute | solution.py:831
  52.0 15.8 %collective-permute-start.15 = (bf16[2,224,128]{2,1,0:T(8,128)(2,1)}, bf16[2,224,128]{2,1,0:T(8,128)(2,1)S(1)}, u32[]{:S(2)}, u32[]{:S(2)}) collective-permute-start(bf16[2,224,128]{2,1,0:T(8,128)(2,1)} %get-tuple-element.192), channel_id=1, source_target_pairs={{0,4},{2,6},{4,0},{6,2},{1,5},{3,7},{5,1},{7,3},{8,12},{10,14},{12... | collective-permute-start | bytes 344072 | tf_op jit(solution)/shard_map/ppermute | solution.py:831
  64.9 22.9 %collective-permute-start.10 = (bf16[2,224,128]{2,1,0:T(8,128)(2,1)}, bf16[2,224,128]{2,1,0:T(8,128)(2,1)S(1)}, u32[]{:S(2)}, u32[]{:S(2)}) collective-permute-start(bf16[2,224,128]{2,1,0:T(8,128)(2,1)} %get-tuple-element.185), channel_id=1, source_target_pairs={{0,2},{2,4},{4,6},{6,0},{1,3},{3,5},{5,7},{7,1},{8,10},{10,12},{12... | collective-permute-start | bytes 344072 | tf_op jit(solution)/shard_map/ppermute | solution.py:831
  66.6 23.5 %collective-permute-start.11 = (bf16[2,224,128]{2,1,0:T(8,128)(2,1)}, bf16[2,224,128]{2,1,0:T(8,128)(2,1)S(1)}, u32[]{:S(2)}, u32[]{:S(2)}) collective-permute-start(bf16[2,224,128]{2,1,0:T(8,128)(2,1)} %get-tuple-element.186), channel_id=1, source_target_pairs={{0,4},{2,6},{4,0},{6,2},{1,5},{3,7},{5,1},{7,3},{8,12},{10,14},{12... | collective-permute-start | bytes 344072 | tf_op jit(solution)/shard_map/ppermute | solution.py:831
  67.8 23.0 %collective-permute-start.12 = (bf16[2,224,128]{2,1,0:T(8,128)(2,1)}, bf16[2,224,128]{2,1,0:T(8,128)(2,1)S(1)}, u32[]{:S(2)}, u32[]{:S(2)}) collective-permute-start(bf16[2,224,128]{2,1,0:T(8,128)(2,1)} %get-tuple-element.187), channel_id=1, source_target_pairs={{0,6},{2,0},{4,2},{6,4},{1,7},{3,1},{5,3},{7,5},{8,14},{10,8},{12,... | collective-permute-start | bytes 344072 | tf_op jit(solution)/shard_map/ppermute | solution.py:831
  85.3 21.3 %collective-permute-start.17 = (bf16[2,224,128]{2,1,0:T(8,128)(2,1)}, bf16[2,224,128]{2,1,0:T(8,128)(2,1)S(1)}, u32[]{:S(2)}, u32[]{:S(2)}) collective-permute-start(bf16[2,224,128]{2,1,0:T(8,128)(2,1)} %get-tuple-element.203), channel_id=1, source_target_pairs={{0,2},{2,4},{4,6},{6,0},{1,3},{3,5},{5,7},{7,1},{8,10},{10,12},{12... | collective-permute-start | bytes 344072 | tf_op jit(solution)/shard_map/ppermute | solution.py:831
  86.1 22.0 %collective-permute-start.18 = (bf16[2,224,128]{2,1,0:T(8,128)(2,1)}, bf16[2,224,128]{2,1,0:T(8,128)(2,1)S(1)}, u32[]{:S(2)}, u32[]{:S(2)}) collective-permute-start(bf16[2,224,128]{2,1,0:T(8,128)(2,1)} %get-tuple-element.204), channel_id=1, source_target_pairs={{0,4},{2,6},{4,0},{6,2},{1,5},{3,7},{5,1},{7,3},{8,12},{10,14},{12... | collective-permute-start | bytes 344072 | tf_op jit(solution)/shard_map/ppermute | solution.py:831
  87.8 22.8 %collective-permute-start.19 = (bf16[2,224,128]{2,1,0:T(8,128)(2,1)}, bf16[2,224,128]{2,1,0:T(8,128)(2,1)S(1)}, u32[]{:S(2)}, u32[]{:S(2)}) collective-permute-start(bf16[2,224,128]{2,1,0:T(8,128)(2,1)} %get-tuple-element.205), channel_id=1, source_target_pairs={{0,6},{2,0},{4,2},{6,4},{1,7},{3,1},{5,3},{7,5},{8,14},{10,8},{12,... | collective-permute-start | bytes 344072 | tf_op jit(solution)/shard_map/ppermute | solution.py:831
  90.2 21.9 %collective-permute-start.20 = (bf16[2,2,224,128]{3,2,1,0:T(8,128)(2,1)}, bf16[2,2,224,128]{3,2,1,0:T(8,128)(2,1)S(1)}, u32[]{:S(2)}, u32[]{:S(2)}) collective-permute-start(bf16[2,2,224,128]{3,2,1,0:T(8,128)(2,1)} %get-tuple-element.207), channel_id=1, source_target_pairs={{0,1},{1,0},{2,3},{3,2},{4,5},{5,4},{6,7},{7,6},{8,9},{9,8},{10,11... | collective-permute-start | bytes 688136 | tf_op jit(solution)/shard_map/ppermute | solution.py:836
  106.6 33.3 %collective-permute-start.21 = (bf16[2,224,128]{2,1,0:T(8,128)(2,1)}, bf16[2,224,128]{2,1,0:T(8,128)(2,1)S(1)}, u32[]{:S(2)}, u32[]{:S(2)}) collective-permute-start(bf16[2,224,128]{2,1,0:T(8,128)(2,1)} %get-tuple-element.220), channel_id=1, source_target_pairs={{0,2},{2,4},{4,6},{6,0},{1,3},{3,5},{5,7},{7,1},{8,10},{10,12},{12... | collective-permute-start | bytes 344072 | tf_op jit(solution)/shard_map/ppermute | solution.py:831
  106.7 33.2 %collective-permute-start.22 = (bf16[2,224,128]{2,1,0:T(8,128)(2,1)}, bf16[2,224,128]{2,1,0:T(8,128)(2,1)S(1)}, u32[]{:S(2)}, u32[]{:S(2)}) collective-permute-start(bf16[2,224,128]{2,1,0:T(8,128)(2,1)} %get-tuple-element.221), channel_id=1, source_target_pairs={{0,4},{2,6},{4,0},{6,2},{1,5},{3,7},{5,1},{7,3},{8,12},{10,14},{12... | collective-permute-start | bytes 344072 | tf_op jit(solution)/shard_map/ppermute | solution.py:831
  108.0 31.9 %collective-permute-start.23 = (bf16[2,224,128]{2,1,0:T(8,128)(2,1)}, bf16[2,224,128]{2,1,0:T(8,128)(2,1)S(1)}, u32[]{:S(2)}, u32[]{:S(2)}) collective-permute-start(bf16[2,224,128]{2,1,0:T(8,128)(2,1)} %get-tuple-element.222), channel_id=1, source_target_pairs={{0,6},{2,0},{4,2},{6,4},{1,7},{3,1},{5,3},{7,5},{8,14},{10,8},{12,... | collective-permute-start | bytes 344072 | tf_op jit(solution)/shard_map/ppermute | solution.py:831
  110.6 29.3 %collective-permute-start.24 = (bf16[2,2,224,128]{3,2,1,0:T(8,128)(2,1)}, bf16[2,2,224,128]{3,2,1,0:T(8,128)(2,1)S(1)}, u32[]{:S(2)}, u32[]{:S(2)}) collective-permute-start(bf16[2,2,224,128]{3,2,1,0:T(8,128)(2,1)} %get-tuple-element.224), channel_id=1, source_target_pairs={{0,1},{1,0},{2,3},{3,2},{4,5},{5,4},{6,7},{7,6},{8,9},{9,8},{10,11... | collective-permute-start | bytes 688136 | tf_op jit(solution)/shard_map/ppermute | solution.py:836
  112.1 30.4 %all-to-all-start = ((bf16[8,32,2304]{2,1,0:T(8,128)(2,1)}), bf16[8,32,2304]{2,1,0:T(8,128)(2,1)S(1)}, u32[]{:S(2)}, u32[]{:S(2)}) async-start(bf16[8,32,2304]{2,1,0:T(8,128)(2,1)} %bitcast.49), calls=%async_computation | async-start | bytes 2359296 | tf_op jit(solution)/shard_map/all_to_all | solution.py:867
  137.8 24.2 %collective-permute-start.28 = (bf16[2,2,224,256]{3,2,1,0:T(8,128)(2,1)}, bf16[2,2,224,256]{3,2,1,0:T(8,128)(2,1)S(1)}, u32[]{:S(2)}, u32[]{:S(2)}) collective-permute-start(bf16[2,2,224,256]{3,2,1,0:T(8,128)(2,1)} %get-tuple-element.239), channel_id=1, source_target_pairs={{0,1},{1,0},{2,3},{3,2},{4,5},{5,4},{6,7},{7,6},{8,9},{9,8},{10,11... | collective-permute-start | bytes 1376264 | tf_op jit(solution)/shard_map/ppermute | solution.py:836
  142.7 21.7 %collective-permute-start.27 = (bf16[32,2304]{1,0:T(8,128)(2,1)S(1)}, bf16[32,2304]{1,0:T(8,128)(2,1)S(1)}, u32[]{:S(2)}, u32[]{:S(2)}) collective-permute-start(bf16[32,2304]{1,0:T(8,128)(2,1)S(1)} %reduce_sum.50), channel_id=1, source_target_pairs={{0,6},{2,0},{4,2},{6,4},{1,7},{3,1},{5,3},{7,5},{8,14},{10,8},{12,... | collective-permute-start | bytes 442376 | tf_op jit(solution)/shard_map/ppermute | solution.py:884
  143.1 22.9 %collective-permute-start.26 = (bf16[32,2304]{1,0:T(8,128)(2,1)S(1)}, bf16[32,2304]{1,0:T(8,128)(2,1)S(1)}, u32[]{:S(2)}, u32[]{:S(2)}) collective-permute-start(bf16[32,2304]{1,0:T(8,128)(2,1)S(1)} %reduce_sum.50), channel_id=1, source_target_pairs={{0,4},{2,6},{4,0},{6,2},{1,5},{3,7},{5,1},{7,3},{8,12},{10,14},{12... | collective-permute-start | bytes 442376 | tf_op jit(solution)/shard_map/ppermute | solution.py:884
  144.6 21.4 %collective-permute-start.25 = (bf16[32,2304]{1,0:T(8,128)(2,1)S(1)}, bf16[32,2304]{1,0:T(8,128)(2,1)S(1)}, u32[]{:S(2)}, u32[]{:S(2)}) collective-permute-start(bf16[32,2304]{1,0:T(8,128)(2,1)S(1)} %reduce_sum.50), channel_id=1, source_target_pairs={{0,2},{2,4},{4,6},{6,0},{1,3},{3,5},{5,7},{7,1},{8,10},{10,12},{12... | collective-permute-start | bytes 442376 | tf_op jit(solution)/shard_map/ppermute | solution.py:884
  161.5 25.1 %collective-permute-start.29 = (bf16[2,224,256]{2,1,0:T(8,128)(2,1)}, bf16[2,224,256]{2,1,0:T(8,128)(2,1)S(1)}, u32[]{:S(2)}, u32[]{:S(2)}) collective-permute-start(bf16[2,224,256]{2,1,0:T(8,128)(2,1)} %get-tuple-element.253), channel_id=1, source_target_pairs={{0,2},{2,4},{4,6},{6,0},{1,3},{3,5},{5,7},{7,1},{8,10},{10,12},{12... | collective-permute-start | bytes 688136 | tf_op jit(solution)/shard_map/ppermute | solution.py:831
  162.0 25.0 %collective-permute-start.30 = (bf16[2,224,256]{2,1,0:T(8,128)(2,1)}, bf16[2,224,256]{2,1,0:T(8,128)(2,1)S(1)}, u32[]{:S(2)}, u32[]{:S(2)}) collective-permute-start(bf16[2,224,256]{2,1,0:T(8,128)(2,1)} %get-tuple-element.254), channel_id=1, source_target_pairs={{0,4},{2,6},{4,0},{6,2},{1,5},{3,7},{5,1},{7,3},{8,12},{10,14},{12... | collective-permute-start | bytes 688136 | tf_op jit(solution)/shard_map/ppermute | solution.py:831
  164.3 22.6 %collective-permute-start.31 = (bf16[2,224,256]{2,1,0:T(8,128)(2,1)}, bf16[2,224,256]{2,1,0:T(8,128)(2,1)S(1)}, u32[]{:S(2)}, u32[]{:S(2)}) collective-permute-start(bf16[2,224,256]{2,1,0:T(8,128)(2,1)} %get-tuple-element.255), channel_id=1, source_target_pairs={{0,6},{2,0},{4,2},{6,4},{1,7},{3,1},{5,3},{7,5},{8,14},{10,8},{12,... | collective-permute-start | bytes 688136 | tf_op jit(solution)/shard_map/ppermute | solution.py:831
  167.1 19.4 %all-to-all-start.1 = ((bf16[8,32,2304]{2,1,0:T(8,128)(2,1)}), bf16[8,32,2304]{2,1,0:T(8,128)(2,1)S(1)}, u32[]{:S(2)}, u32[]{:S(2)}) async-start(bf16[8,32,2304]{2,1,0:T(8,128)(2,1)} %broadcast_in_dim.60), calls=%async_computation.1 | async-start | bytes 2359296 | tf_op jit(solution)/shard_map/all_to_all | solution.py:879
  177.7 15.0 %collective-permute-start.32 = (bf16[2,224,256]{2,1,0:T(8,128)(2,1)}, bf16[2,224,256]{2,1,0:T(8,128)(2,1)S(1)}, u32[]{:S(2)}, u32[]{:S(2)}) collective-permute-start(bf16[2,224,256]{2,1,0:T(8,128)(2,1)} %get-tuple-element.258), channel_id=1, source_target_pairs={{0,2},{2,4},{4,6},{6,0},{1,3},{3,5},{5,7},{7,1},{8,10},{10,12},{12... | collective-permute-start | bytes 688136 | tf_op jit(solution)/shard_map/ppermute | solution.py:831
  199.3 38.9 %all-to-all-start.2 = ((bf16[32,8,896]{2,1,0:T(8,128)(2,1)}), bf16[32,8,896]{2,1,0:T(8,128)(2,1)S(1)}, u32[]{:S(2)}, u32[]{:S(2)}) async-start(bf16[32,8,896]{2,1,0:T(8,128)(2,1)} %bitcast.50), calls=%async_computation.2 | async-start | bytes 917504 | tf_op jit(solution)/shard_map/all_to_all | solution.py:867
  223.2 17.6 %collective-permute-start.35 = (bf16[2,2,224,256]{3,2,1,0:T(8,128)(2,1)}, bf16[2,2,224,256]{3,2,1,0:T(8,128)(2,1)S(1)}, u32[]{:S(2)}, u32[]{:S(2)}) collective-permute-start(bf16[2,2,224,256]{3,2,1,0:T(8,128)(2,1)} %get-tuple-element.272), channel_id=1, source_target_pairs={{0,1},{1,0},{2,3},{3,2},{4,5},{5,4},{6,7},{7,6},{8,9},{9,8},{10,11... | collective-permute-start | bytes 1376264 | tf_op jit(solution)/shard_map/ppermute | solution.py:836
  241.7 19.7 %all-to-all-start.3 = ((bf16[32,8,896]{2,1,0:T(8,128)(2,1)}), bf16[32,8,896]{2,1,0:T(8,128)(2,1)S(1)}, u32[]{:S(2)}, u32[]{:S(2)}) async-start(bf16[32,8,896]{2,1,0:T(8,128)(2,1)} %broadcast_in_dim.61), calls=%async_computation.3 | async-start | bytes 917504 | tf_op jit(solution)/shard_map/all_to_all | solution.py:879
  (51 other events, 386.1 us)
where the time goes:
time: 268 us; the launch traced here: 265 us
  Pallas kernels  104 us (39%)
  starting transfers between devices  97.6 us (36%)
  local copies, waits for them, and re-layouts  30.6 us (11%)
  waiting for transfers between devices  29.5 us (11%)
    pallas_call x14, Pallas kernels, call(): pl.pallas_call(body, out_shape=[shape for unused, shape in outputs], grid...  104 us
    all_to_all x2, starting transfers between devices, send_shares(): return lax.all_to_all(sent, axes, 0, 0)  38.4 us
    ppermute x24, starting transfers between devices, row_exchange(): lax.ppermute(parts[k], 'row', [(q, (q + k) % size) for q in range(size)])  35.8 us
    unnamed x91, local copies, waits for them, and re-layouts  19.5 us
    all_to_all x2, waiting for transfers between devices, send_shares(): return lax.all_to_all(sent, axes, 0, 0)  9.95 us
    ppermute x7, starting transfers between devices, col_exchange(): return [keep, lax.ppermute(send, 'col', [(0, 1), (1, 0)])]  9.52 us
    all_to_all x2, waiting for transfers between devices, gather_spread(): return lax.all_to_all(sent, axes, 0, 0).reshape((-1,) + sent.shape[2:])  8.99 us
    all_to_all x2, starting transfers between devices, gather_spread(): return lax.all_to_all(sent, axes, 0, 0).reshape((-1,) + sent.shape[2:])  8.36 us
  transfers between devices with their start and end apart: 40, of which 7 were waited for; matrix products, arithmetic and copies ran while one was open for 7% of the time, Pallas kernels for 38%

commit v1 on v0

--- a/solution.py
+++ b/solution.py
@@ -241,7 +241,7 @@
 DOWN_GRID = (4 * ROWS, SLOT, HALF)
 ACROSS_GRID = (2, 8, STRIPE, SLOT, HALF)
 DOWN_SIZES = (640, 768, 896)
-ACROSS_SIZES = (336, 448)
+ACROSS_SIZES = (280, 336, 392, 448)
 DOWN_GROUP = 4
 MIDDLE_GROUP = 4
 HIDDEN_TILE = 512
@@ -498,45 +498,58 @@
         g = g_ref[where].reshape(size, DIM)
         mixed = nn(joined, wm_ref[...]) + bm_ref[...]
         middle = x + scale_attend * mixed
-        hat, rstd = normalize(middle)
-        normed = (hat * gain_ref[...] + shift_ref[...]).astype(BF16)
-        d_reduced = (scale_feed * g).astype(BF16)
-        turned_grad, turned_normed = d_reduced.T, normed.T
-        tiles = HIDDEN // HIDDEN_TILE
-        first_dots, hidden = {}, {}
-        reduced, d_normed, sums = br_ref[...], 0.0, []
-        for t in range(tiles + 2):
-            if t < tiles:
-                cols = slice(HIDDEN_TILE * t, HIDDEN_TILE * t + HIDDEN_TILE)
-                first_dots[t] = nn(normed, we_ref[:, cols]), nt(d_reduced, wr_ref[cols])
-            if 1 <= t <= tiles:
-                j = t - 1
-                cols = slice(HIDDEN_TILE * j, HIDDEN_TILE * j + HIDDEN_TILE)
-                pre, d_act = first_dots.pop(j)
-                hidden[j] = gelu_pair(pre + be_ref[:, cols], d_act)
-            if t >= 2:
-                j = t - 2
-                cols = slice(HIDDEN_TILE * j, HIDDEN_TILE * j + HIDDEN_TILE)
-                wide_cols = slice(HIDDEN + HIDDEN_TILE * j, HIDDEN + HIDDEN_TILE * j + HIDDEN_TILE)
-                act, d_hidden = hidden.pop(j)
-                reduced = reduced + nn(act, wr_ref[cols])
-                d_normed = d_normed + nt(d_hidden, we_ref[:, cols])
-                acc[:, cols] += nn(turned_grad, act)
-                acc[:, wide_cols] += nn(turned_normed, d_hidden)
-                sums.append(col_sum(d_hidden.astype(F32)))
-        d_hidden_sum = jnp.concatenate(sums, axis=1)
-        o_ref[where] = (middle + scale_feed * reduced).reshape(group, ROWS, SLOT, DIM)
-        d_middle = g + norm_back(d_normed * gain_ref[...], hat, rstd)
-        dm_ref[0, where] = d_middle.astype(BF16).reshape(group, PIX, DIM)
-        d_mixed = (scale_attend * d_middle).astype(BF16)
-        acc[:, 2 * HIDDEN :] += tn(joined, d_mixed)
-        dj_ref[where] = nt(d_mixed, wm_ref[...]).reshape(group, ROWS, SLOT, DIM)
-        rows = [d_hidden_sum[:, DIM * k : DIM * k + DIM] for k in range(4)]
-        rows.append(col_sum(d_reduced.astype(F32)))
-        rows.append(col_sum(d_normed * hat))
-        rows.append(col_sum(d_normed))
-        rows.append(col_sum(d_mixed.astype(F32)))
-        acc_v[...] += jnp.concatenate(rows, axis=0)
+        def mixing_back(d_middle):
+            dm_ref[0, where] = d_middle.astype(BF16).reshape(group, PIX, DIM)
+            d_mixed = (scale_attend * d_middle).astype(BF16)
+            acc[:, 2 * HIDDEN :] += tn(joined, d_mixed)
+            dj_ref[where] = nt(d_mixed, wm_ref[...]).reshape(group, ROWS, SLOT, DIM)
+            acc_v[7:8] += col_sum(d_mixed.astype(F32))
+
+        fed = meta.feed(i) > 0
+
+        @pl.when(fed)
+        def _():
+            hat, rstd = normalize(middle)
+            normed = (hat * gain_ref[...] + shift_ref[...]).astype(BF16)
+            d_reduced = (scale_feed * g).astype(BF16)
+            turned_grad, turned_normed = d_reduced.T, normed.T
+            tiles = HIDDEN // HIDDEN_TILE
+            first_dots, hidden = {}, {}
+            reduced, d_normed, sums = br_ref[...], 0.0, []
+            for t in range(tiles + 2):
+                if t < tiles:
+                    cols = slice(HIDDEN_TILE * t, HIDDEN_TILE * t + HIDDEN_TILE)
+                    first_dots[t] = nn(normed, we_ref[:, cols]), nt(d_reduced, wr_ref[cols])
+                if 1 <= t <= tiles:
+                    j = t - 1
+                    cols = slice(HIDDEN_TILE * j, HIDDEN_TILE * j + HIDDEN_TILE)
+                    pre, d_act = first_dots.pop(j)
+                    hidden[j] = gelu_pair(pre + be_ref[:, cols], d_act)
+                if t >= 2:
+                    j = t - 2
+                    cols = slice(HIDDEN_TILE * j, HIDDEN_TILE * j + HIDDEN_TILE)
+                    wide_cols = slice(HIDDEN + HIDDEN_TILE * j, HIDDEN + HIDDEN_TILE * j + HIDDEN_TILE)
+                    act, d_hidden = hidden.pop(j)
+                    reduced = reduced + nn(act, wr_ref[cols])
+                    d_normed = d_normed + nt(d_hidden, we_ref[:, cols])
+                    acc[:, cols] += nn(turned_grad, act)
+                    acc[:, wide_cols] += nn(turned_normed, d_hidden)
+                    sums.append(col_sum(d_hidden.astype(F32)))
+            d_hidden_sum = jnp.concatenate(sums, axis=1)
+            o_ref[where] = (middle + scale_feed * reduced).reshape(group, ROWS, SLOT, DIM)
+            d_middle = g + norm_back(d_normed * gain_ref[...], hat, rstd)
+            mixing_back(d_middle)
+            rows = [d_hidden_sum[:, DIM * k : DIM * k + DIM] for k in range(4)]
+            rows.append(col_sum(d_reduced.astype(F32)))
+            rows.append(col_sum(d_normed * hat))
+            rows.append(col_sum(d_normed))
+            acc_v[0:7] += jnp.concatenate(rows, axis=0)
+
+        @pl.when(jnp.logical_not(fed))
+        def _():
+            o_ref[where] = middle.reshape(group, ROWS, SLOT, DIM)
+            mixing_back(g)
+
         return carry
 
     lax.fori_loop(0, 4 // group, one, 0)
@@ -849,12 +862,9 @@
     return found
 
 
-def kept_total(flags):
-    total = flags
+def kept_step(total, bit):
     size = lax.axis_size("batch")
-    for bit in bits_of(size):
-        total = total + lax.ppermute(total, "batch", [(q, q ^ bit) for q in range(size)])
-    return total
+    return total + lax.ppermute(total, "batch", [(q, q ^ bit) for q in range(size)])
 
 
 ALL = ("batch", "row", "col")
@@ -961,7 +971,11 @@
     own0, keep_flags, triple_weight, query_value_bias, position_kernel = together(
         own0, keep_flags, triple_weight, query_value_bias, position_kernel
     )
-    kept = kept_total(jnp.sum(keep_flags.astype(F32), axis=0))
+    kept = jnp.sum(keep_flags.astype(F32), axis=0)
+    for step, bit in enumerate(bits_of(lax.axis_size("batch"))):
+        kept = kept_step(kept, bit)
+        if step == 0:
+            own0, kept = together(own0, kept)
     share = kept / (count * lax.axis_size("batch"))
     factors = (keep_flags.astype(F32) / share).reshape(-1)
 

time: 268 us -> 284 us (1.060)
  starting transfers between devices: 97.6 us -> 110 us
  Pallas kernels: 104 us -> 115 us
  waiting for transfers between devices: 29.5 us -> 20.8 us
    pallas_call x14, Pallas kernels: 104 us -> 115 us  [call(): pl.pallas_call(body, out_shape=[shape for unused, shape in outputs], grid...]
    ppermute x24, starting transfers between devices: 35.8 us -> 45.1 us  [row_exchange(): lax.ppermute(parts[k], 'row', [(q, (q + k) % size) for q in range(size)])]
    all_to_all x2, starting transfers between devices: 8.36 us -> 17.5 us  [gather_spread(): return lax.all_to_all(sent, axes, 0, 0).reshape((-1,) + sent.shape[2:])]
    all_to_all x2, starting transfers between devices: 38.4 us -> 30.8 us  [send_shares(): return lax.all_to_all(sent, axes, 0, 0)]
    all_to_all x2, waiting for transfers between devices: 8.99 us -> 5.05 us  [gather_spread(): return lax.all_to_all(sent, axes, 0, 0).reshape((-1,) + sent.shape[2:])]
    unnamed x91 -> x97, local copies, waits for them, and re-layouts: 19.5 us -> 19.5 us
  transfers between devices with their start and end apart: 40 -> 40, of which waited for: 7 -> 6; matrix products, arithmetic and copies ran while one was open for 7% -> 7% of each run, Pallas kernels for 38% -> 40%
where the time goes in v1:
time: 284 us; the launch traced here: 280 us
  Pallas kernels  115 us (40%)
  starting transfers between devices  110 us (39%)
  local copies, waits for them, and re-layouts  30.6 us (11%)
  waiting for transfers between devices  20.8 us (7%)
    pallas_call x14, Pallas kernels, call(): pl.pallas_call(body, out_shape=[shape for unused, shape in outputs], grid...  115 us
    ppermute x24, starting transfers between devices, row_exchange(): lax.ppermute(parts[k], 'row', [(q, (q + k) % size) for q in range(size)])  45.1 us
    all_to_all x2, starting transfers between devices, send_shares(): return lax.all_to_all(sent, axes, 0, 0)  30.8 us
    unnamed x97, local copies, waits for them, and re-layouts  19.5 us
    all_to_all x2, starting transfers between devices, gather_spread(): return lax.all_to_all(sent, axes, 0, 0).reshape((-1,) + sent.shape[2:])  17.5 us
    ppermute x7, starting transfers between devices, col_exchange(): return [keep, lax.ppermute(send, 'col', [(0, 1), (1, 0)])]  10.5 us
    all_to_all x2, waiting for transfers between devices, send_shares(): return lax.all_to_all(sent, axes, 0, 0)  9.97 us
  transfers between devices with their start and end apart: 40, of which 6 were waited for; matrix products, arithmetic and copies ran while one was open for 7% of the time, Pallas kernels for 40%

profile of v1, /device:TPU:0, one launch (start us, length us, event | category | flops | bytes accessed | tf_op | source)
XLA Modules:
  0.0 279.7 jit_solution(11423663212379527578)
XLA Ops:
  1.4 3.0 %copy.54.refs_1_ = bf16[4,28,28,256]{3,2,1,0:T(8,128)(2,1)} copy(bf16[4,28,28,256]{3,0,2,1:T(4,128)(2,1)} %param.19) | data formatting | bytes 3211264 | tf_op args[0]
  5.1 3.3 %prep.2 = (bf16[2,224,256]{2,1,0:T(8,128)(2,1)}, bf16[2,224,256]{2,1,0:T(8,128)(2,1)}, bf16[2,224,256]{2,1,0:T(8,128)(2,1)}, bf16[2,224,256]{2,1,0:T(8,128)(2,1)...) custom-call(s32[18]{0:T(128)} %concatenate.15.refs_0_, bf16[4,28,28,256]{3,2,1,0:T(8,128)(2,1)} %copy.54.refs_1_), custom_call_target="tpu_custom_call" | custom-call | flops 4000000000 | bytes 1605632 | tf_op jit(solution)/shard_map/prep/pallas_call | solution.py:810
  9.0 2.6 collective-permute-start.2
  19.5 2.6 collective-permute-start.8
  24.3 3.2 %prep.3 = (bf16[2,224,256]{2,1,0:T(8,128)(2,1)}, bf16[2,224,256]{2,1,0:T(8,128)(2,1)}, bf16[2,224,256]{2,1,0:T(8,128)(2,1)}, bf16[2,224,256]{2,1,0:T(8,128)(2,1)...) custom-call(s32[18]{0:T(128)} %concatenate.15.refs_0_, bf16[4,28,28,256]{3,2,1,0:T(8,128)(2,1)} %copy.54.refs_1_, ...), custom_call_target="tpu_custom_call" | custom-call | flops 4000000000 | bytes 1605632 | tf_op jit(solution)/shard_map/prep/pallas_call | solution.py:810
  28.2 7.1 %across_forward.2 = (bf16[4,2,224,128]{3,2,1,0:T(8,128)(2,1)}, bf16[4,2,224,128]{3,2,1,0:T(8,128)(2,1)}, bf16[4,896,128]{2,1,0:T(8,128)(2,1)}, bf16[4,896,128]{2...) custom-call(s32[18]{0:T(128)} %concatenate.15.refs_0_, ...), custom_call_target="tpu_custom_call" | custom-call | flops 10000000000 | bytes 1135104 | tf_op jit(solution)/shard_map/across_forward/pallas_call | solution.py:810
  36.4 3.4 %collective-permute-start.5 = (bf16[2,224,256]{2,1,0:T(8,128)(2,1)S(1)}, bf16[2,224,256]{2,1,0:T(8,128)(2,1)S(1)}, u32[]{:S(2)}, u32[]{:S(2)}) collective-permute-start(bf16[2,224,256]{2,1,0:T(8,128)(2,1)S(1)} %copy-done.24), channel_id=1, source_target_pairs={{0,6},{2,0},{4,2},{6,4},{1,7},{3,1},{5,3},{7,5},{8,14},{10,8},{12,... | collective-permute-start | bytes 688136 | tf_op jit(solution)/shard_map/ppermute | solution.py:844
  41.2 8.5 %down_forward.2 = (bf16[2,224,128]{2,1,0:T(8,128)(2,1)}, bf16[2,224,128]{2,1,0:T(8,128)(2,1)}, bf16[2,224,128]{2,1,0:T(8,128)(2,1)}, bf16[2,224,128]{2,1,0:T(8,1...) custom-call(s32[18]{0:T(128)} %concatenate.15.refs_0_, ...), custom_call_target="tpu_custom_call" | custom-call | flops 12000000000 | bytes 1135104 | tf_op jit(solution)/shard_map/down_forward/pallas_call | solution.py:810
  49.7 12.2 %collective-permute-start.14 = (bf16[2,224,128]{2,1,0:T(8,128)(2,1)}, bf16[2,224,128]{2,1,0:T(8,128)(2,1)S(1)}, u32[]{:S(2)}, u32[]{:S(2)}) collective-permute-start(bf16[2,224,128]{2,1,0:T(8,128)(2,1)} %get-tuple-element.201), channel_id=1, source_target_pairs={{0,2},{2,4},{4,6},{6,0},{1,3},{3,5},{5,7},{7,1},{8,10},{10,12},{12... | collective-permute-start | bytes 344072 | tf_op jit(solution)/shard_map/ppermute | solution.py:844
  61.9 3.3 %collective-permute-start.15 = (bf16[2,224,128]{2,1,0:T(8,128)(2,1)}, bf16[2,224,128]{2,1,0:T(8,128)(2,1)S(1)}, u32[]{:S(2)}, u32[]{:S(2)}) collective-permute-start(bf16[2,224,128]{2,1,0:T(8,128)(2,1)} %get-tuple-element.202), channel_id=1, source_target_pairs={{0,4},{2,6},{4,0},{6,2},{1,5},{3,7},{5,1},{7,3},{8,12},{10,14},{12... | collective-permute-start | bytes 344072 | tf_op jit(solution)/shard_map/ppermute | solution.py:844
  65.2 7.2 %across_forward.3 = (bf16[4,2,224,128]{3,2,1,0:T(8,128)(2,1)}, bf16[4,2,224,128]{3,2,1,0:T(8,128)(2,1)}, bf16[4,896,128]{2,1,0:T(8,128)(2,1)}, bf16[4,896,128]{2...) custom-call(s32[18]{0:T(128)} %concatenate.15.refs_0_, ...), custom_call_target="tpu_custom_call", output_to_operand_aliasing={{0}: (9, {}), {1}: (10, {}), {2}: (11, {}), {3}: (12, {}), ... | custom-call | flops 10000000000 | bytes 1135104 | tf_op jit(solution)/shard_map/across_forward/pallas_call | solution.py:810
  74.6 6.8 %down_forward.3 = (bf16[2,224,128]{2,1,0:T(8,128)(2,1)}, bf16[2,224,128]{2,1,0:T(8,128)(2,1)}, bf16[2,224,128]{2,1,0:T(8,128)(2,1)}, bf16[2,224,128]{2,1,0:T(8,1...) custom-call(s32[18]{0:T(128)} %concatenate.15.refs_0_, ...), custom_call_target="tpu_custom_call" | custom-call | flops 12000000000 | bytes 1135104 | tf_op jit(solution)/shard_map/down_forward/pallas_call | solution.py:810
  86.9 11.2 %middle.2 = (bf16[4,28,28,256]{3,2,1,0:T(8,128)(2,1)}, bf16[4,4,224,256]{3,2,1,0:T(8,128)(2,1)}, bf16[2,224,128]{2,1,0:T(8,128)(2,1)}, bf16[2,224,128]{2,1,0:T(8...) custom-call(s32[18]{0:T(128)} %concatenate.15.refs_0_, ...), custom_call_target="tpu_custom_call" | custom-call | flops 16000000000 | bytes 5087232 | tf_op jit(solution)/shard_map/middle/pallas_call | solution.py:810
  104.3 11.3 %middle.3 = (bf16[4,28,28,256]{3,2,1,0:T(8,128)(2,1)}, bf16[4,4,224,256]{3,2,1,0:T(8,128)(2,1)}, bf16[2,224,128]{2,1,0:T(8,128)(2,1)}, bf16[2,224,128]{2,1,0:T(8...) custom-call(s32[18]{0:T(128)} %concatenate.15.refs_0_, ...), custom_call_target="tpu_custom_call", output_to_operand_aliasing={{0}: (23, {}), {1}: (24, {})} | custom-call | flops 16000000000 | bytes 6275072 | tf_op jit(solution)/shard_map/middle/pallas_call | solution.py:810
  117.2 2.8 %collective-permute-start.23 = (bf16[2,224,128]{2,1,0:T(8,128)(2,1)}, bf16[2,224,128]{2,1,0:T(8,128)(2,1)S(1)}, u32[]{:S(2)}, u32[]{:S(2)}) collective-permute-start(bf16[2,224,128]{2,1,0:T(8,128)(2,1)} %get-tuple-element.232), channel_id=1, source_target_pairs={{0,6},{2,0},{4,2},{6,4},{1,7},{3,1},{5,3},{7,5},{8,14},{10,8},{12,... | collective-permute-start | bytes 344072 | tf_op jit(solution)/shard_map/ppermute | solution.py:844
  121.4 11.7 %all-to-all-start = ((bf16[8,32,2304]{2,1,0:T(8,128)(2,1)}), bf16[8,32,2304]{2,1,0:T(8,128)(2,1)S(1)}, u32[]{:S(2)}, u32[]{:S(2)}) async-start(bf16[8,32,2304]{2,1,0:T(8,128)(2,1)} %bitcast.49), calls=%async_computation | async-start | bytes 2359296 | tf_op jit(solution)/shard_map/all_to_all | solution.py:877
  133.2 11.2 %across_backward.2 = (bf16[2,2,224,256]{3,2,1,0:T(8,128)(2,1)}, bf16[2,2,224,256]{3,2,1,0:T(8,128)(2,1)}, f32[272,768]{1,0:T(8,128)}) custom-call(s32[18]{0:T(128)} %concatenate.15.refs_0_, bf16[2,2,224,256]{3,2,1,0:T(8,128)(2,1)} %get-tuple-element.169.refs_1_, bf16[2,2,224,256]{3,2,1,0:T(8,128)(2,1)} %copy-done.8, ...), custom_call_target="tpu_custom_call" | custom-call | flops 17999998976 | bytes 5376000 | tf_op jit(solution)/shard_map/across_backward/pallas_call | solution.py:810
  146.5 2.6 all-to-all-done
  153.0 15.1 %down_backward.2 = (bf16[2,224,256]{2,1,0:T(8,128)(2,1)}, bf16[2,224,256]{2,1,0:T(8,128)(2,1)}, bf16[2,224,256]{2,1,0:T(8,128)(2,1)}, bf16[2,224,256]{2,1,0:T(8,128)(2,1)}, f32[272,768]{1,0:T(8,128)}) custom-call(s32[18]{0:T(128)} %concatenate.15.refs_0_, bf16[2,224,256]{2,1,0:T(8,128)(2,1)} %get-tuple-element.188.refs_1_.refs_2_, ...), custom_call_target="tpu_custom_call" | custom-call | flops 22000001024 | bytes 4319232 | tf_op jit(solution)/shard_map/down_backward/pallas_call | solution.py:810
  173.5 12.7 %all-to-all-start.1 = ((bf16[8,32,2304]{2,1,0:T(8,128)(2,1)}), bf16[8,32,2304]{2,1,0:T(8,128)(2,1)S(1)}, u32[]{:S(2)}, u32[]{:S(2)}) async-start(bf16[8,32,2304]{2,1,0:T(8,128)(2,1)} %broadcast_in_dim.60), calls=%async_computation.1 | async-start | bytes 2359296 | tf_op jit(solution)/shard_map/all_to_all | solution.py:889
  186.2 12.0 %down_backward.3 = (bf16[2,224,256]{2,1,0:T(8,128)(2,1)}, bf16[2,224,256]{2,1,0:T(8,128)(2,1)}, bf16[2,224,256]{2,1,0:T(8,128)(2,1)}, bf16[2,224,256]{2,1,0:T(8,128)(2,1)}, f32[272,768]{1,0:T(8,128)}) custom-call(s32[18]{0:T(128)} %concatenate.15.refs_0_, bf16[2,224,256]{2,1,0:T(8,128)(2,1)} %get-tuple-element.175.refs_9_.refs_1_.refs_2_, ...), custom_call_target="tpu_custom_call" | custom-call | flops 22000001024 | bytes 4319232 | tf_op jit(solution)/shard_map/down_backward/pallas_call | solution.py:810
  199.2 3.3 %all-to-all-done.1 = bf16[8,32,2304]{2,1,0:T(8,128)(2,1)S(1)} async-done(((bf16[8,32,2304]{2,1,0:T(8,128)(2,1)}), bf16[8,32,2304]{2,1,0:T(8,128)(2,1)S(1)}, u32[]{:S(2)}, u32[]{:S(2)}) %all-to-all-start.1) | async-done | bytes 1179680 | tf_op jit(solution)/shard_map/all_to_all | solution.py:889
  203.7 11.2 %across_backward.3 = (bf16[2,2,224,256]{3,2,1,0:T(8,128)(2,1)}, bf16[2,2,224,256]{3,2,1,0:T(8,128)(2,1)}, bf16[256,896]{1,0:T(8,128)(2,1)}) custom-call(s32[18]{0:T(128)} %concatenate.15.refs_0_, bf16[2,2,224,256]{3,2,1,0:T(8,128)(2,1)} %get-tuple-element.179.refs_1_, bf16[2,2,224,256]{3,2,1,0:T(8,128)(2,1)} %copy-done.7, ...), custom_call_target="tpu_custom_call" | custom-call | flops 17999998976 | bytes 6219776 | tf_op jit(solution)/shard_map/across_backward/pallas_call | solution.py:810
  214.9 3.1 %collective-permute-done.33.refs_4_ = bf16[2,224,256]{2,1,0:T(8,128)(2,1)S(1)} collective-permute-done((bf16[2,224,256]{2,1,0:T(8,128)(2,1)}, bf16[2,224,256]{2,1,0:T(8,128)(2,1)S(1)}, u32[]{:S(2)}, u32[]{:S(2)}) %collective-permute-start.33) | collective-permute-done | bytes 229408 | tf_op jit(solution)/shard_map/ppermute | solution.py:844
  218.7 19.1 %all-to-all-start.2 = ((bf16[32,8,896]{2,1,0:T(8,128)(2,1)}), bf16[32,8,896]{2,1,0:T(8,128)(2,1)S(1)}, u32[]{:S(2)}, u32[]{:S(2)}) async-start(bf16[32,8,896]{2,1,0:T(8,128)(2,1)} %bitcast.50), calls=%async_computation.2 | async-start | bytes 917504 | tf_op jit(solution)/shard_map/all_to_all | solution.py:877
  241.8 3.6 %finish.2.refs_8_ = bf16[4,28,28,256]{3,2,1,0:T(8,128)(2,1)} custom-call(s32[18]{0:T(128)} %concatenate.15.refs_0_, bf16[4,4,224,256]{3,2,1,0:T(8,128)(2,1)} %get-tuple-element.210.refs_1_, bf16[2,224,256]{2,1,0:T(8,128)(2,1)} %get-tuple-element.278.refs_2_, bf16[2,224,256]{2,1,0:T(8,128)(2,1)} %copy-done.26, bf16[2,224,256]{2,1,0:T(8,128)(2,1)} %copy-done.27, ...), custom_call_target="tpu_custom_call" | custom-call | flops 4000000000 | bytes 3670016 | tf_op jit(solution)/shard_map/finish/pallas_call | solution.py:810
  245.4 7.4 %all-to-all-done.2 = bf16[32,8,896]{2,1,0:T(8,128)(2,1)S(1)} async-done(((bf16[32,8,896]{2,1,0:T(8,128)(2,1)}), bf16[32,8,896]{2,1,0:T(8,128)(2,1)S(1)}, u32[]{:S(2)}, u32[]{:S(2)}) %all-to-all-start.2) | async-done | bytes 458784 | tf_op jit(solution)/shard_map/all_to_all | solution.py:877
  252.9 2.6 collective-permute-done.35.refs_7_
  256.4 4.8 %all-to-all-start.3 = ((bf16[32,8,896]{2,1,0:T(8,128)(2,1)}), bf16[32,8,896]{2,1,0:T(8,128)(2,1)S(1)}, u32[]{:S(2)}, u32[]{:S(2)}) async-start(bf16[32,8,896]{2,1,0:T(8,128)(2,1)} %broadcast_in_dim.61), calls=%async_computation.3 | async-start | bytes 917504 | tf_op jit(solution)/shard_map/all_to_all | solution.py:889
  261.1 4.1 %copy.59 = bf16[4,28,28,256]{3,0,2,1:T(4,128)(2,1)} copy(bf16[4,28,28,256]{3,2,1,0:T(8,128)(2,1)} %get-tuple-element.306) | data formatting | bytes 3211264
  265.3 3.6 %finish.3 = bf16[4,28,28,256]{3,2,1,0:T(8,128)(2,1)} custom-call(s32[18]{0:T(128)} %concatenate.15.refs_0_, bf16[4,4,224,256]{3,2,1,0:T(8,128)(2,1)} %get-tuple-element.210.refs_1_, bf16[2,224,256]{2,1,0:T(8,128)(2,1)} %get-tuple-element.272.refs_2_, bf16[2,224,256]{2,1,0:T(8,128)(2,1)} %copy-done.29, ...), custom_call_target="tpu_custom_call", output_to_operand_aliasing={{}: (8, {})} | custom-call | flops 4000000000 | bytes 3670016 | tf_op jit(solution)/shard_map/finish/pallas_call | solution.py:810
  268.9 4.1 %copy.60 = bf16[4,28,28,256]{3,0,2,1:T(4,128)(2,1)} copy(bf16[4,28,28,256]{3,2,1,0:T(8,128)(2,1)} %finish.3) | data formatting | bytes 3211264
  (194 shorter events, 57.6 us)
Async XLA Ops:
  9.0 18.4 %collective-permute-start.2 = (bf16[2,2,224,256]{3,2,1,0:T(8,128)(2,1)}, bf16[2,2,224,256]{3,2,1,0:T(8,128)(2,1)S(1)}, u32[]{:S(2)}, u32[]{:S(2)}) collective-permute-start(bf16[2,2,224,256]{3,2,1,0:T(8,128)(2,1)} %get-tuple-element.170), channel_id=1, source_target_pairs={{0,1},{1,0},{2,3},{3,2},{4,5},{5,4},{6,7},{7,6},{8,9},{9,8},{10,11... | collective-permute-start | bytes 1376264 | tf_op jit(solution)/shard_map/ppermute | solution.py:849
  18.0 18.5 %collective-permute-start.7 = (bf16[2,224,256]{2,1,0:T(8,128)(2,1)S(1)}, bf16[2,224,256]{2,1,0:T(8,128)(2,1)S(1)}, u32[]{:S(2)}, u32[]{:S(2)}) collective-permute-start(bf16[2,224,256]{2,1,0:T(8,128)(2,1)S(1)} %copy-done.19), channel_id=1, source_target_pairs={{0,2},{2,4},{4,6},{6,0},{1,3},{3,5},{5,7},{7,1},{8,10},{10,12},{12... | collective-permute-start | bytes 688136 | tf_op jit(solution)/shard_map/ppermute | solution.py:844
  19.5 20.3 %collective-permute-start.8 = (bf16[2,224,256]{2,1,0:T(8,128)(2,1)S(1)}, bf16[2,224,256]{2,1,0:T(8,128)(2,1)S(1)}, u32[]{:S(2)}, u32[]{:S(2)}) collective-permute-start(bf16[2,224,256]{2,1,0:T(8,128)(2,1)S(1)} %copy-done.20), channel_id=1, source_target_pairs={{0,4},{2,6},{4,0},{6,2},{1,5},{3,7},{5,1},{7,3},{8,12},{10,14},{12... | collective-permute-start | bytes 688136 | tf_op jit(solution)/shard_map/ppermute | solution.py:844
  22.1 18.3 %collective-permute-start.9 = (bf16[2,224,256]{2,1,0:T(8,128)(2,1)S(1)}, bf16[2,224,256]{2,1,0:T(8,128)(2,1)S(1)}, u32[]{:S(2)}, u32[]{:S(2)}) collective-permute-start(bf16[2,224,256]{2,1,0:T(8,128)(2,1)S(1)} %copy-done.21), channel_id=1, source_target_pairs={{0,6},{2,0},{4,2},{6,4},{1,7},{3,1},{5,3},{7,5},{8,14},{10,8},{12,... | collective-permute-start | bytes 688136 | tf_op jit(solution)/shard_map/ppermute | solution.py:844
  35.4 37.1 %collective-permute-start.3 = (bf16[2,224,256]{2,1,0:T(8,128)(2,1)S(1)}, bf16[2,224,256]{2,1,0:T(8,128)(2,1)S(1)}, u32[]{:S(2)}, u32[]{:S(2)}) collective-permute-start(bf16[2,224,256]{2,1,0:T(8,128)(2,1)S(1)} %copy-done.22), channel_id=1, source_target_pairs={{0,2},{2,4},{4,6},{6,0},{1,3},{3,5},{5,7},{7,1},{8,10},{10,12},{12... | collective-permute-start | bytes 688136 | tf_op jit(solution)/shard_map/ppermute | solution.py:844
  36.1 36.4 %collective-permute-start.4 = (bf16[2,224,256]{2,1,0:T(8,128)(2,1)S(1)}, bf16[2,224,256]{2,1,0:T(8,128)(2,1)S(1)}, u32[]{:S(2)}, u32[]{:S(2)}) collective-permute-start(bf16[2,224,256]{2,1,0:T(8,128)(2,1)S(1)} %copy-done.23), channel_id=1, source_target_pairs={{0,4},{2,6},{4,0},{6,2},{1,5},{3,7},{5,1},{7,3},{8,12},{10,14},{12... | collective-permute-start | bytes 688136 | tf_op jit(solution)/shard_map/ppermute | solution.py:844
  36.4 37.5 %collective-permute-start.5 = (bf16[2,224,256]{2,1,0:T(8,128)(2,1)S(1)}, bf16[2,224,256]{2,1,0:T(8,128)(2,1)S(1)}, u32[]{:S(2)}, u32[]{:S(2)}) collective-permute-start(bf16[2,224,256]{2,1,0:T(8,128)(2,1)S(1)} %copy-done.24), channel_id=1, source_target_pairs={{0,6},{2,0},{4,2},{6,4},{1,7},{3,1},{5,3},{7,5},{8,14},{10,8},{12,... | collective-permute-start | bytes 688136 | tf_op jit(solution)/shard_map/ppermute | solution.py:844
  39.9 22.1 %collective-permute-start.6 = (bf16[2,2,224,256]{3,2,1,0:T(8,128)(2,1)S(1)}, bf16[2,2,224,256]{3,2,1,0:T(8,128)(2,1)S(1)}, u32[]{:S(2)}, u32[]{:S(2)}) collective-permute-start(bf16[2,2,224,256]{3,2,1,0:T(8,128)(2,1)S(1)} %copy-done.11), channel_id=1, source_target_pairs={{0,1},{1,0},{2,3},{3,2},{4,5},{5,4},{6,7},{7,6},{8,9},{9,8},{10,11... | collective-permute-start | bytes 1376264 | tf_op jit(solution)/shard_map/ppermute | solution.py:849
  49.7 33.7 %collective-permute-start.14 = (bf16[2,224,128]{2,1,0:T(8,128)(2,1)}, bf16[2,224,128]{2,1,0:T(8,128)(2,1)S(1)}, u32[]{:S(2)}, u32[]{:S(2)}) collective-permute-start(bf16[2,224,128]{2,1,0:T(8,128)(2,1)} %get-tuple-element.201), channel_id=1, source_target_pairs={{0,2},{2,4},{4,6},{6,0},{1,3},{3,5},{5,7},{7,1},{8,10},{10,12},{12... | collective-permute-start | bytes 344072 | tf_op jit(solution)/shard_map/ppermute | solution.py:844
  61.9 22.3 %collective-permute-start.15 = (bf16[2,224,128]{2,1,0:T(8,128)(2,1)}, bf16[2,224,128]{2,1,0:T(8,128)(2,1)S(1)}, u32[]{:S(2)}, u32[]{:S(2)}) collective-permute-start(bf16[2,224,128]{2,1,0:T(8,128)(2,1)} %get-tuple-element.202), channel_id=1, source_target_pairs={{0,4},{2,6},{4,0},{6,2},{1,5},{3,7},{5,1},{7,3},{8,12},{10,14},{12... | collective-permute-start | bytes 344072 | tf_op jit(solution)/shard_map/ppermute | solution.py:844
  81.4 19.3 %collective-permute-start.10 = (bf16[2,224,128]{2,1,0:T(8,128)(2,1)}, bf16[2,224,128]{2,1,0:T(8,128)(2,1)S(1)}, u32[]{:S(2)}, u32[]{:S(2)}) collective-permute-start(bf16[2,224,128]{2,1,0:T(8,128)(2,1)} %get-tuple-element.195), channel_id=1, source_target_pairs={{0,2},{2,4},{4,6},{6,0},{1,3},{3,5},{5,7},{7,1},{8,10},{10,12},{12... | collective-permute-start | bytes 344072 | tf_op jit(solution)/shard_map/ppermute | solution.py:844
  83.4 19.5 %collective-permute-start.11 = (bf16[2,224,128]{2,1,0:T(8,128)(2,1)}, bf16[2,224,128]{2,1,0:T(8,128)(2,1)S(1)}, u32[]{:S(2)}, u32[]{:S(2)}) collective-permute-start(bf16[2,224,128]{2,1,0:T(8,128)(2,1)} %get-tuple-element.196), channel_id=1, source_target_pairs={{0,4},{2,6},{4,0},{6,2},{1,5},{3,7},{5,1},{7,3},{8,12},{10,14},{12... | collective-permute-start | bytes 344072 | tf_op jit(solution)/shard_map/ppermute | solution.py:844
  84.2 19.4 %collective-permute-start.12 = (bf16[2,224,128]{2,1,0:T(8,128)(2,1)}, bf16[2,224,128]{2,1,0:T(8,128)(2,1)S(1)}, u32[]{:S(2)}, u32[]{:S(2)}) collective-permute-start(bf16[2,224,128]{2,1,0:T(8,128)(2,1)} %get-tuple-element.197), channel_id=1, source_target_pairs={{0,6},{2,0},{4,2},{6,4},{1,7},{3,1},{5,3},{7,5},{8,14},{10,8},{12,... | collective-permute-start | bytes 344072 | tf_op jit(solution)/shard_map/ppermute | solution.py:844
  98.6 18.7 %collective-permute-start.18 = (bf16[2,224,128]{2,1,0:T(8,128)(2,1)}, bf16[2,224,128]{2,1,0:T(8,128)(2,1)S(1)}, u32[]{:S(2)}, u32[]{:S(2)}) collective-permute-start(bf16[2,224,128]{2,1,0:T(8,128)(2,1)} %get-tuple-element.214), channel_id=1, source_target_pairs={{0,4},{2,6},{4,0},{6,2},{1,5},{3,7},{5,1},{7,3},{8,12},{10,14},{12... | collective-permute-start | bytes 344072 | tf_op jit(solution)/shard_map/ppermute | solution.py:844
  100.7 19.4 %collective-permute-start.19 = (bf16[2,224,128]{2,1,0:T(8,128)(2,1)}, bf16[2,224,128]{2,1,0:T(8,128)(2,1)S(1)}, u32[]{:S(2)}, u32[]{:S(2)}) collective-permute-start(bf16[2,224,128]{2,1,0:T(8,128)(2,1)} %get-tuple-element.215), channel_id=1, source_target_pairs={{0,6},{2,0},{4,2},{6,4},{1,7},{3,1},{5,3},{7,5},{8,14},{10,8},{12,... | collective-permute-start | bytes 344072 | tf_op jit(solution)/shard_map/ppermute | solution.py:844
  103.0 18.5 %collective-permute-start.20 = (bf16[2,2,224,128]{3,2,1,0:T(8,128)(2,1)}, bf16[2,2,224,128]{3,2,1,0:T(8,128)(2,1)S(1)}, u32[]{:S(2)}, u32[]{:S(2)}) collective-permute-start(bf16[2,2,224,128]{3,2,1,0:T(8,128)(2,1)} %get-tuple-element.217), channel_id=1, source_target_pairs={{0,1},{1,0},{2,3},{3,2},{4,5},{5,4},{6,7},{7,6},{8,9},{9,8},{10,11... | collective-permute-start | bytes 688136 | tf_op jit(solution)/shard_map/ppermute | solution.py:849
  115.6 30.8 %collective-permute-start.21 = (bf16[2,224,128]{2,1,0:T(8,128)(2,1)}, bf16[2,224,128]{2,1,0:T(8,128)(2,1)S(1)}, u32[]{:S(2)}, u32[]{:S(2)}) collective-permute-start(bf16[2,224,128]{2,1,0:T(8,128)(2,1)} %get-tuple-element.230), channel_id=1, source_target_pairs={{0,2},{2,4},{4,6},{6,0},{1,3},{3,5},{5,7},{7,1},{8,10},{10,12},{12... | collective-permute-start | bytes 344072 | tf_op jit(solution)/shard_map/ppermute | solution.py:844
  115.8 30.6 %collective-permute-start.22 = (bf16[2,224,128]{2,1,0:T(8,128)(2,1)}, bf16[2,224,128]{2,1,0:T(8,128)(2,1)S(1)}, u32[]{:S(2)}, u32[]{:S(2)}) collective-permute-start(bf16[2,224,128]{2,1,0:T(8,128)(2,1)} %get-tuple-element.231), channel_id=1, source_target_pairs={{0,4},{2,6},{4,0},{6,2},{1,5},{3,7},{5,1},{7,3},{8,12},{10,14},{12... | collective-permute-start | bytes 344072 | tf_op jit(solution)/shard_map/ppermute | solution.py:844
  117.2 29.2 %collective-permute-start.23 = (bf16[2,224,128]{2,1,0:T(8,128)(2,1)}, bf16[2,224,128]{2,1,0:T(8,128)(2,1)S(1)}, u32[]{:S(2)}, u32[]{:S(2)}) collective-permute-start(bf16[2,224,128]{2,1,0:T(8,128)(2,1)} %get-tuple-element.232), channel_id=1, source_target_pairs={{0,6},{2,0},{4,2},{6,4},{1,7},{3,1},{5,3},{7,5},{8,14},{10,8},{12,... | collective-permute-start | bytes 344072 | tf_op jit(solution)/shard_map/ppermute | solution.py:844
  120.1 26.4 %collective-permute-start.24 = (bf16[2,2,224,128]{3,2,1,0:T(8,128)(2,1)}, bf16[2,2,224,128]{3,2,1,0:T(8,128)(2,1)S(1)}, u32[]{:S(2)}, u32[]{:S(2)}) collective-permute-start(bf16[2,2,224,128]{3,2,1,0:T(8,128)(2,1)} %get-tuple-element.234), channel_id=1, source_target_pairs={{0,1},{1,0},{2,3},{3,2},{4,5},{5,4},{6,7},{7,6},{8,9},{9,8},{10,11... | collective-permute-start | bytes 688136 | tf_op jit(solution)/shard_map/ppermute | solution.py:849
  121.4 27.6 %all-to-all-start = ((bf16[8,32,2304]{2,1,0:T(8,128)(2,1)}), bf16[8,32,2304]{2,1,0:T(8,128)(2,1)S(1)}, u32[]{:S(2)}, u32[]{:S(2)}) async-start(bf16[8,32,2304]{2,1,0:T(8,128)(2,1)} %bitcast.49), calls=%async_computation | async-start | bytes 2359296 | tf_op jit(solution)/shard_map/all_to_all | solution.py:877
  144.3 24.2 %collective-permute-start.28 = (bf16[2,2,224,256]{3,2,1,0:T(8,128)(2,1)}, bf16[2,2,224,256]{3,2,1,0:T(8,128)(2,1)S(1)}, u32[]{:S(2)}, u32[]{:S(2)}) collective-permute-start(bf16[2,2,224,256]{3,2,1,0:T(8,128)(2,1)} %get-tuple-element.249), channel_id=1, source_target_pairs={{0,1},{1,0},{2,3},{3,2},{4,5},{5,4},{6,7},{7,6},{8,9},{9,8},{10,11... | collective-permute-start | bytes 1376264 | tf_op jit(solution)/shard_map/ppermute | solution.py:849
  149.2 21.6 %collective-permute-start.27 = (bf16[32,2304]{1,0:T(8,128)(2,1)S(1)}, bf16[32,2304]{1,0:T(8,128)(2,1)S(1)}, u32[]{:S(2)}, u32[]{:S(2)}) collective-permute-start(bf16[32,2304]{1,0:T(8,128)(2,1)S(1)} %reduce_sum.50), channel_id=1, source_target_pairs={{0,6},{2,0},{4,2},{6,4},{1,7},{3,1},{5,3},{7,5},{8,14},{10,8},{12,... | collective-permute-start | bytes 442376 | tf_op jit(solution)/shard_map/ppermute | solution.py:894
  149.8 22.5 %collective-permute-start.26 = (bf16[32,2304]{1,0:T(8,128)(2,1)S(1)}, bf16[32,2304]{1,0:T(8,128)(2,1)S(1)}, u32[]{:S(2)}, u32[]{:S(2)}) collective-permute-start(bf16[32,2304]{1,0:T(8,128)(2,1)S(1)} %reduce_sum.50), channel_id=1, source_target_pairs={{0,4},{2,6},{4,0},{6,2},{1,5},{3,7},{5,1},{7,3},{8,12},{10,14},{12... | collective-permute-start | bytes 442376 | tf_op jit(solution)/shard_map/ppermute | solution.py:894
  151.3 21.1 %collective-permute-start.25 = (bf16[32,2304]{1,0:T(8,128)(2,1)S(1)}, bf16[32,2304]{1,0:T(8,128)(2,1)S(1)}, u32[]{:S(2)}, u32[]{:S(2)}) collective-permute-start(bf16[32,2304]{1,0:T(8,128)(2,1)S(1)} %reduce_sum.50), channel_id=1, source_target_pairs={{0,2},{2,4},{4,6},{6,0},{1,3},{3,5},{5,7},{7,1},{8,10},{10,12},{12... | collective-permute-start | bytes 442376 | tf_op jit(solution)/shard_map/ppermute | solution.py:894
  168.1 34.5 %collective-permute-start.29 = (bf16[2,224,256]{2,1,0:T(8,128)(2,1)}, bf16[2,224,256]{2,1,0:T(8,128)(2,1)S(1)}, u32[]{:S(2)}, u32[]{:S(2)}) collective-permute-start(bf16[2,224,256]{2,1,0:T(8,128)(2,1)} %get-tuple-element.263), channel_id=1, source_target_pairs={{0,2},{2,4},{4,6},{6,0},{1,3},{3,5},{5,7},{7,1},{8,10},{10,12},{12... | collective-permute-start | bytes 688136 | tf_op jit(solution)/shard_map/ppermute | solution.py:844
  168.5 34.4 %collective-permute-start.30 = (bf16[2,224,256]{2,1,0:T(8,128)(2,1)}, bf16[2,224,256]{2,1,0:T(8,128)(2,1)S(1)}, u32[]{:S(2)}, u32[]{:S(2)}) collective-permute-start(bf16[2,224,256]{2,1,0:T(8,128)(2,1)} %get-tuple-element.264), channel_id=1, source_target_pairs={{0,4},{2,6},{4,0},{6,2},{1,5},{3,7},{5,1},{7,3},{8,12},{10,14},{12... | collective-permute-start | bytes 688136 | tf_op jit(solution)/shard_map/ppermute | solution.py:844
  170.9 32.1 %collective-permute-start.31 = (bf16[2,224,256]{2,1,0:T(8,128)(2,1)}, bf16[2,224,256]{2,1,0:T(8,128)(2,1)S(1)}, u32[]{:S(2)}, u32[]{:S(2)}) collective-permute-start(bf16[2,224,256]{2,1,0:T(8,128)(2,1)} %get-tuple-element.265), channel_id=1, source_target_pairs={{0,6},{2,0},{4,2},{6,4},{1,7},{3,1},{5,3},{7,5},{8,14},{10,8},{12,... | collective-permute-start | bytes 688136 | tf_op jit(solution)/shard_map/ppermute | solution.py:844
  173.5 29.1 %all-to-all-start.1 = ((bf16[8,32,2304]{2,1,0:T(8,128)(2,1)}), bf16[8,32,2304]{2,1,0:T(8,128)(2,1)S(1)}, u32[]{:S(2)}, u32[]{:S(2)}) async-start(bf16[8,32,2304]{2,1,0:T(8,128)(2,1)} %broadcast_in_dim.60), calls=%async_computation.1 | async-start | bytes 2359296 | tf_op jit(solution)/shard_map/all_to_all | solution.py:889
  198.9 19.1 %collective-permute-start.33 = (bf16[2,224,256]{2,1,0:T(8,128)(2,1)}, bf16[2,224,256]{2,1,0:T(8,128)(2,1)S(1)}, u32[]{:S(2)}, u32[]{:S(2)}) collective-permute-start(bf16[2,224,256]{2,1,0:T(8,128)(2,1)} %get-tuple-element.269), channel_id=1, source_target_pairs={{0,4},{2,6},{4,0},{6,2},{1,5},{3,7},{5,1},{7,3},{8,12},{10,14},{12... | collective-permute-start | bytes 688136 | tf_op jit(solution)/shard_map/ppermute | solution.py:844
  218.7 34.1 %all-to-all-start.2 = ((bf16[32,8,896]{2,1,0:T(8,128)(2,1)}), bf16[32,8,896]{2,1,0:T(8,128)(2,1)S(1)}, u32[]{:S(2)}, u32[]{:S(2)}) async-start(bf16[32,8,896]{2,1,0:T(8,128)(2,1)} %bitcast.50), calls=%async_computation.2 | async-start | bytes 917504 | tf_op jit(solution)/shard_map/all_to_all | solution.py:877
  256.4 19.7 %all-to-all-start.3 = ((bf16[32,8,896]{2,1,0:T(8,128)(2,1)}), bf16[32,8,896]{2,1,0:T(8,128)(2,1)S(1)}, u32[]{:S(2)}, u32[]{:S(2)}) async-start(bf16[32,8,896]{2,1,0:T(8,128)(2,1)} %broadcast_in_dim.61), calls=%async_computation.3 | async-start | bytes 917504 | tf_op jit(solution)/shard_map/all_to_all | solution.py:889
  (54 other events, 390.8 us)
